TPU v7x, 256 devices: a whole 4x4x8 slice. The times are simulated.
256 devices in a mesh: group: 16 (over z, core), dev: 16 (over y, x).
Axes of the slice: x: 4, y: 4, z: 8, core: 2. Of those that a mesh axis runs over, the one named last changes fastest.
Arguments:
- memory: bfloat16 [65536, 512], P(('group', 'dev')), may hold values from -3 to 3
- event_features: bfloat16 [131072, 172], P(('group', 'dev')), may hold values from -6 to 6
- event_dest: int32 [131072, 1], P(('group', 'dev')), may hold values from 0 to 15; in each aligned block of 512 rows (0 to 511, 512 to 1023, ...) at most 96 rows name the same one
- event_slot: int32 [131072], P(('group', 'dev')), may hold values from 0 to 255
- neighbours: int32 [65536, 20], P(('group', 'dev')), may hold values from 0 to 65535, as said below
- w_message: bfloat16 [172, 512], replicated, may hold values from -0.4375 to 0.4375
- w_input: bfloat16 [512, 1536], replicated, may hold values from -0.25 to 0.25
- w_hidden: bfloat16 [512, 1536], replicated, may hold values from -0.25 to 0.25
- w_query: bfloat16 [512, 512], replicated
- w_keyval: bfloat16 [512, 1024], replicated, may hold values from -0.25 to 0.25
- w_output: bfloat16 [512, 512], replicated, may hold values from -0.25 to 0.25
Outputs:
- new_memory: bfloat16 [65536, 512], P(('group', 'dev'))
- embedding: bfloat16 [65536, 512], P(('group', 'dev'))
Inputs may be any that keep to these rules, and one draw needn't show every extreme that they name: `event_dest`: every device's 512 events send at most 96 events to one owner, and exactly 96 to some owner. Each cell's neighbours lie in its own range of 4096 cells or in one of the two adjacent ranges, the last range being adjacent to the first. The 5120 entries of one device's cells name cells of each of the 48 owners of these three ranges equally often, up to one, so that no owner is named more than 107 times and some owner exactly 107 times.
All inputs are finite; a program needn't handle non-finite values.
Results may differ from a plain program's by a relative error of at most 0.017.
The roundings to bfloat16 on the way count: a program that leaves them out, or rounds other values in their place, can miss the bound.
Values may be sent and summed in bfloat16 or wider, within the bound.
A program may use at most 128 MiB of HBM per device.

v0:
```python
import jax
import jax.numpy as jnp
from jax import lax
from jax.sharding import PartitionSpec as P

HEADS = 8


def extended(cells, sides, width):
    for axis, dim in sides:
        count = lax.axis_size(axis)
        head = lax.slice_in_dim(cells, 0, width, axis=dim)
        tail = lax.slice_in_dim(cells, cells.shape[dim] - width, cells.shape[dim], axis=dim)
        cells = jnp.concatenate(
            [
                lax.ppermute(tail, axis, [(i, (i + 1) % count) for i in range(count)]),
                cells,
                lax.ppermute(head, axis, [((i + 1) % count, i) for i in range(count)]),
            ],
            axis=dim,
        )
    return cells


def as_float(values):
    return values.astype(jnp.float32)


def body(
    memory,
    event_features,
    event_dest,
    event_slot,
    neighbours,
    w_message,
    w_input,
    w_hidden,
    w_query,
    w_keyval,
    w_output,
):
    owners = lax.axis_size("dev")
    ranges_all = lax.axis_size("group")
    events = event_features.shape[0]
    slots = 3 * events // owners
    cells = memory.shape[0]
    width = memory.shape[1]
    count_nbr = neighbours.shape[1]
    head_size = width // HEADS
    dest = event_dest[:, 0]
    onehot = (dest[:, None] == jnp.arange(owners, dtype=jnp.int32)[None, :]).astype(jnp.int32)
    before = jnp.cumsum(onehot, axis=0) - onehot
    place = dest * slots + jnp.sum(before * onehot, axis=1)
    marks = (
        jnp.zeros((owners * slots,), jnp.int32).at[place].set(event_slot + 1).reshape(owners, slots)
    )
    feat_width = event_features.shape[1]
    packed = (
        jnp.zeros((owners * slots, feat_width), jnp.bfloat16)
        .at[place]
        .set(event_features)
        .reshape(owners, slots, feat_width)
    )
    received, got_marks = (
        lax.all_to_all(packed, "dev", split_axis=0, concat_axis=0, tiled=True),
        lax.all_to_all(marks, "dev", split_axis=0, concat_axis=0, tiled=True),
    )
    arrived = jax.nn.silu(
        jnp.dot(
            received.reshape(owners * slots, feat_width),
            w_message,
            preferred_element_type=jnp.float32,
        )
    ).astype(jnp.bfloat16)
    target = got_marks.reshape(-1) - 1
    table = (jnp.arange(cells, dtype=jnp.int32)[:, None] == target[None, :]).astype(jnp.bfloat16)
    sums = jnp.dot(table, arrived, preferred_element_type=jnp.float32)
    counts = jnp.sum(table.astype(jnp.float32), axis=1)
    mean_msg = (sums / jnp.maximum(counts, 1.0)[:, None]).astype(jnp.bfloat16)
    gi = jnp.dot(mean_msg, w_input, preferred_element_type=jnp.float32)
    gh = jnp.dot(memory, w_hidden, preferred_element_type=jnp.float32)
    zgate = jax.nn.sigmoid(gi[:, :width] + gh[:, :width])
    rgate = jax.nn.sigmoid(gi[:, width : 2 * width] + gh[:, width : 2 * width])
    cand = jnp.tanh(gi[:, 2 * width :] + rgate * gh[:, 2 * width :])
    old = memory.astype(jnp.float32)
    updated = (1.0 - zgate) * old + zgate * cand
    new_memory = jnp.where(counts[:, None] > 0, updated, old).astype(jnp.bfloat16)
    range_cells = cells * owners
    flat_ids = neighbours.reshape(-1)
    which = (flat_ids // range_cells - lax.axis_index("group") + 1 + ranges_all) % ranges_all
    within = flat_ids % range_cells
    local_ids = which * range_cells + within
    block = lax.all_gather(new_memory, "dev", axis=0, tiled=True)
    spread = extended(block, (("group", 0),), range_cells)
    picked = jnp.take(spread, local_ids, axis=0)
    keyval = jnp.dot(picked, w_keyval, preferred_element_type=jnp.float32).astype(jnp.bfloat16)
    keyval = keyval.reshape(cells, count_nbr, 2 * width)
    query = (
        jnp.dot(new_memory, w_query, preferred_element_type=jnp.float32)
        / jnp.sqrt(jnp.float32(head_size))
    ).astype(jnp.bfloat16)
    keys = keyval[:, :, :width].reshape(cells, count_nbr, HEADS, head_size)
    values = keyval[:, :, width:].reshape(cells, count_nbr, HEADS, head_size)
    qheads = query.reshape(cells, HEADS, head_size)
    scores = jnp.einsum("bhd,bnhd->bhn", qheads, keys, preferred_element_type=jnp.float32)
    attn_w = jax.nn.softmax(scores, axis=-1).astype(jnp.bfloat16)
    attended = (
        jnp.einsum("bhn,bnhd->bhd", attn_w, values, preferred_element_type=jnp.float32)
        .reshape(cells, width)
        .astype(jnp.bfloat16)
    )
    embedding = (
        as_float(new_memory) + jnp.dot(attended, w_output, preferred_element_type=jnp.float32)
    ).astype(jnp.bfloat16)
    return (new_memory, embedding)


def solution(mesh):
    placed = (
        P(("group", "dev"), None),
        P(("group", "dev"), None),
        P(("group", "dev"), None),
        P(("group", "dev")),
        P(("group", "dev"), None),
        P(),
        P(),
        P(),
        P(),
        P(),
        P(),
    )
    return jax.shard_map(
        body,
        mesh=mesh,
        in_specs=placed,
        out_specs=(P(("group", "dev"), None), P(("group", "dev"), None)),
        check_vma=False,
    )
```

profile of v0, /device:TPU:97, one launch (start us, length us, event | category | flops | bytes accessed | tf_op | source)
XLA Modules:
  0.0 278.1 jit_solution(2177651143755832187)
XLA Ops:
  7.2 0.8 fusion.33
  8.0 1.1 reduce-window.6
  9.4 0.8 fusion.32
  10.2 0.7 compare_select_fusion.7
  10.9 0.7 broadcast_add_fusion
  11.5 2.4 scatter_custom_fusion
  14.7 6.8 %all-to-all-start = ((s32[16,1,96]{2,1,0:T(1,128)}), s32[16,1,96]{2,1,0:T(1,128)S(1)}, u32[]{:S(2)}, u32[]{:S(2)}) async-start(s32[16,1,96]{2,1,0:T(1,128)} %all_to_all.9), calls=%async_computation | async-start | bytes 16384 | tf_op jit(solution)/shard_map/all_to_all | solution.py:66
  21.5 1.5 fusion.47
  23.0 1.1 copy.38
  24.0 2.6 scatter_custom_fusion.1
  26.6 1.2 copy.39
  27.8 6.7 %all-to-all-start.1 = ((bf16[16,96,172]{1,2,0:T(8,128)(2,1)}), bf16[16,96,172]{1,2,0:T(8,128)(2,1)S(1)}, u32[]{:S(2)}, u32[]{:S(2)}) async-start(bf16[16,96,172]{1,2,0:T(8,128)(2,1)} %copy.39), calls=%async_computation.1 | async-start | bytes 1441792 | tf_op jit(solution)/shard_map/all_to_all | solution.py:65
  34.9 11.7 %all-to-all-done.1 = bf16[16,96,172]{1,2,0:T(8,128)(2,1)S(1)} async-done(((bf16[16,96,172]{1,2,0:T(8,128)(2,1)}), bf16[16,96,172]{1,2,0:T(8,128)(2,1)S(1)}, u32[]{:S(2)}, u32[]{:S(2)}) %all-to-all-start.1) | async-done | bytes 528416 | tf_op jit(solution)/shard_map/all_to_all | solution.py:65
  46.8 0.8 reshape.225
  47.6 2.2 multiply_convert_fusion
  49.9 3.0 %fusion.9 = f32[256,1536]{1,0:T(8,128)S(1)} fusion(bf16[512,1536]{1,0:T(8,128)(2,1)} %param.17, bf16[1536,512]{1,0:T(8,128)(2,1)} %multiply_convert_fusion, s32[1536]{0:T(1024)S(1)} %sub.49, f32[256]{0:T(256)S(1)} %broadcast_maximum_fusion), kind=kOutput, calls=%fused_computation.21 | convolution fusion | flops 805961728 | bytes 4725760 | tf_op jit(solution)/shard_map/dot_general | solution.py:80
  52.9 1.1 fusion.13
  53.9 56.6 %all-gather.2.cloned.1.call-done = bf16[4096,512]{1,0:T(8,128)(2,1)} async-done(((bf16[256,512]{1,0:T(8,128)(2,1)}), bf16[4096,512]{1,0:T(8,128)(2,1)}) %all-gather.2.cloned.1.call-update) | async-done | bytes 4194320 | tf_op jit(solution)/shard_map/all_gather | solution.py:93
  110.5 3.0 %collective-permute-start = (bf16[4096,512]{1,0:T(8,128)(2,1)}, bf16[4096,512]{1,0:T(8,128)(2,1)}, u32[]{:S(2)}, u32[]{:S(2)}) collective-permute-start(bf16[4096,512]{1,0:T(8,128)(2,1)} %all-gather.2.cloned.1.call-done), channel_id=1, source_target_pairs={{0,16},{16,32},{32,48},{48,64},{64,80},{80,96},{96,112},{112,128},... | collective-permute-start | bytes 12582920 | tf_op jit(solution)/shard_map/ppermute | solution.py:16
  114.3 1.4 fusion.6
  115.9 43.4 %collective-permute-done = bf16[4096,512]{1,0:T(8,128)(2,1)} collective-permute-done((bf16[4096,512]{1,0:T(8,128)(2,1)}, bf16[4096,512]{1,0:T(8,128)(2,1)}, u32[]{:S(2)}, u32[]{:S(2)}) %collective-permute-start) | collective-permute-done | bytes 4194336 | tf_op jit(solution)/shard_map/ppermute | solution.py:16
  159.3 3.7 %collective-permute-done.1 = bf16[4096,512]{1,0:T(8,128)(2,1)} collective-permute-done((bf16[4096,512]{1,0:T(8,128)(2,1)}, bf16[4096,512]{1,0:T(8,128)(2,1)}, u32[]{:S(2)}, u32[]{:S(2)}) %collective-permute-start.1) | collective-permute-done | bytes 4194336 | tf_op jit(solution)/shard_map/ppermute | solution.py:18
  163.0 15.9 %pad_maximum_fusion = bf16[12288,512]{1,0:T(8,128)(2,1)} fusion(bf16[4096,512]{1,0:T(8,128)(2,1)} %collective-permute-done.1, bf16[4096,512]{1,0:T(8,128)(2,1)} %all-gather.2.cloned.1.call-done, bf16[4096,512]{1,0:T(8,128)(2,1)} %collective-permute-done), kind=kLoop, calls=%fused_computation.3 | loop fusion | flops 37748736 | bytes 25165824 | tf_op jit(solution)/shard_map/concatenate | solution.py:14
  178.9 27.8 %gather_fusion = bf16[5120,512]{1,0:T(8,128)(2,1)} fusion(bf16[12288,512]{1,0:T(8,128)(2,1)} %pad_maximum_fusion, s32[5120]{0:T(1024)S(1)} %broadcast_clamp_fusion), kind=kCustom, calls=%fused_computation | custom fusion | bytes 10506240 | tf_op jit(solution)/shard_map/jit(_take)/gather | solution.py:95
  206.7 11.2 %convolution_convert_fusion = bf16[5120,1024]{1,0:T(8,128)(2,1)} fusion(bf16[512,1024]{1,0:T(8,128)(2,1)S(1)} %copy-done.6, bf16[5120,512]{1,0:T(8,128)(2,1)} %gather_fusion, pred[5120]{0:T(1024)(128)(4,1)S(1)} %compare_and_fusion), kind=kOutput, calls=%fused_computation.6 | convolution fusion | flops 5376573440 | bytes 16782336 | tf_op jit(solution)/shard_map/dot_general | solution.py:96
  217.9 16.3 %reshape.229 = bf16[256,20,1024]{2,1,0:T(8,128)(2,1)} reshape(bf16[5120,1024]{1,0:T(8,128)(2,1)} %convolution_convert_fusion) | data formatting | bytes 20971520 | tf_op jit(solution)/shard_map/reshape | solution.py:97
  234.3 10.3 %fusion.46 = (bf16[256,20,512]{2,1,0:T(8,128)(2,1)}, bf16[256,20,512]{2,1,0:T(8,128)(2,1)}) fusion(bf16[256,20,1024]{2,1,0:T(8,128)(2,1)} %reshape.229), kind=kLoop, calls=%fused_computation.96 | loop fusion | bytes 20971520 | tf_op jit(solution)/shard_map/slice | solution.py:102
  244.5 8.6 %copy.57 = bf16[256,20,512]{0,2,1:T(8,128)(2,1)} copy(bf16[256,20,512]{2,1,0:T(8,128)(2,1)} %get-tuple-element.2) | data formatting | bytes 10485760
  253.1 4.4 %multiply_reduce_fusion.1 = f32[256,8,20]{0,1,2:T(8,128)S(1)} fusion(f32[256,8,64]{0,2,1:T(8,128)S(1)} %bitcast_convert_fusion, bf16[256,20,512]{0,2,1:T(8,128)(2,1)} %copy.57), kind=kLoop, calls=%fused_computation.5 | loop fusion | flops 7823360 | bytes 5931008 | tf_op jit(solution)/shard_map/bhd,bnhd->bhn/dot_general | solution.py:105
  257.6 8.7 %copy.58 = bf16[256,20,512]{0,2,1:T(8,128)(2,1)} copy(bf16[256,20,512]{2,1,0:T(8,128)(2,1)} %get-tuple-element.3) | data formatting | bytes 10485760
  266.4 3.8 %multiply_reduce_fusion = bf16[256,8,64]{0,2,1:T(8,128)(2,1)S(1)} fusion(bf16[256,8,20,64]{0,3,1,2:T(8,128)(2,1)} %bitcast.50, f32[256,8,20]{0,1,2:T(8,128)S(1)} %fusion.29), kind=kLoop, calls=%fused_computation.4 | loop fusion | flops 7733248 | bytes 5668864 | tf_op jit(solution)/shard_map/bhn,bnhd->bhd/dot_general | solution.py:108
  270.2 1.0 fusion.7
  (41 shorter events, 2.5 us)
Async XLA Ops:
  7.2 14.3 %copy-start = (bf16[512,1536]{1,0:T(8,128)(2,1)S(1)}, bf16[512,1536]{1,0:T(8,128)(2,1)}, u32[]{:S(2)}) copy-start(bf16[512,1536]{1,0:T(8,128)(2,1)} %param.18) | copy-start | bytes 4718596
  8.0 39.6 %copy-start.7 = (bf16[172,512]{1,0:T(8,128)(2,1)S(1)}, bf16[172,512]{1,0:T(8,128)(2,1)}, u32[]{:S(2)}) copy-start(bf16[172,512]{1,0:T(8,128)(2,1)} %param.16) | copy-start | bytes 528388
  14.7 13.1 %all-to-all-start = ((s32[16,1,96]{2,1,0:T(1,128)}), s32[16,1,96]{2,1,0:T(1,128)S(1)}, u32[]{:S(2)}, u32[]{:S(2)}) async-start(s32[16,1,96]{2,1,0:T(1,128)} %all_to_all.9), calls=%async_computation | async-start | bytes 16384 | tf_op jit(solution)/shard_map/all_to_all | solution.py:66
  27.8 18.8 %all-to-all-start.1 = ((bf16[16,96,172]{1,2,0:T(8,128)(2,1)}), bf16[16,96,172]{1,2,0:T(8,128)(2,1)S(1)}, u32[]{:S(2)}, u32[]{:S(2)}) async-start(bf16[16,96,172]{1,2,0:T(8,128)(2,1)} %copy.39), calls=%async_computation.1 | async-start | bytes 1441792 | tf_op jit(solution)/shard_map/all_to_all | solution.py:65
  34.5 76.0 %all-gather.2.cloned.1.call-start = ((), (), s32[]{:S(2)}) async-start(), calls=%async_computation.2 | async-start | bytes 4456448 | tf_op jit(solution)/shard_map/all_gather | solution.py:93
  49.8 3.0 %copy-start.3 = (bf16[256,512]{1,0:T(8,128)(2,1)S(1)}, bf16[256,512]{1,0:T(8,128)(2,1)}, u32[]{:S(2)}) copy-start(bf16[256,512]{1,0:T(8,128)(2,1)} %param.11) | copy-start | bytes 786436
  49.8 63.7 %copy-start.5 = (s32[256,20]{0,1:T(8,128)S(1)}, s32[256,20]{0,1:T(8,128)}, u32[]{:S(2)}) copy-start(s32[256,20]{0,1:T(8,128)} %param.15) | copy-start | bytes 61444
  110.5 48.8 %collective-permute-start = (bf16[4096,512]{1,0:T(8,128)(2,1)}, bf16[4096,512]{1,0:T(8,128)(2,1)}, u32[]{:S(2)}, u32[]{:S(2)}) collective-permute-start(bf16[4096,512]{1,0:T(8,128)(2,1)} %all-gather.2.cloned.1.call-done), channel_id=1, source_target_pairs={{0,16},{16,32},{32,48},{48,64},{64,80},{80,96},{96,112},{112,128},... | collective-permute-start | bytes 12582920 | tf_op jit(solution)/shard_map/ppermute | solution.py:16
  113.6 49.5 %collective-permute-start.1 = (bf16[4096,512]{1,0:T(8,128)(2,1)}, bf16[4096,512]{1,0:T(8,128)(2,1)}, u32[]{:S(2)}, u32[]{:S(2)}) collective-permute-start(bf16[4096,512]{1,0:T(8,128)(2,1)} %all-gather.2.cloned.1.call-done), channel_id=1, source_target_pairs={{16,0},{32,16},{48,32},{64,48},{80,64},{96,80},{112,96},{128,112},... | collective-permute-start | bytes 12582920 | tf_op jit(solution)/shard_map/ppermute | solution.py:18
  178.9 27.8 %copy-start.6 = (bf16[512,1024]{1,0:T(8,128)(2,1)S(1)}, bf16[512,1024]{1,0:T(8,128)(2,1)}, u32[]{:S(2)}) copy-start(bf16[512,1024]{1,0:T(8,128)(2,1)} %param.20) | copy-start | bytes 3145732
  257.6 13.6 %copy-start.1 = (bf16[512,1536]{1,0:T(8,128)(2,1)S(1)}, bf16[512,1536]{1,0:T(8,128)(2,1)}, u32[]{:S(2)}) copy-start(bf16[512,1536]{1,0:T(8,128)(2,1)} %param.18) | copy-start | bytes 4718596
  266.4 3.8 %copy-start.2 = (bf16[256,512]{1,0:T(8,128)(2,1)S(1)}, bf16[256,512]{1,0:T(8,128)(2,1)}, u32[]{:S(2)}) copy-start(bf16[256,512]{1,0:T(8,128)(2,1)} %fusion.13) | copy-start | bytes 786436
  266.4 3.8 %copy-start.4 = (bf16[512,512]{1,0:T(8,128)(2,1)S(1)}, bf16[512,512]{1,0:T(8,128)(2,1)}, u32[]{:S(2)}) copy-start(bf16[512,512]{1,0:T(8,128)(2,1)} %param.21) | copy-start | bytes 1572868
Sparse Core Ops, SparseCore 0:
  54.1 56.4 all-gather.1
where the time goes:
time: 279 us; the launch traced here: 278 us
  waiting for transfers between devices  115 us (41%)
  local copies, waits for them, and re-layouts  81.5 us (29%)
  other arithmetic  29.9 us (11%)
  matrix products  20.3 us (7%)
  starting transfers between devices  16.5 us (6%)
  between operations  14.3 us (5%)
    all_gather x1, waiting for transfers between devices, body(): block = lax.all_gather(new_memory, 'dev', axis=0, tiled=True)  56.6 us
    ppermute x1, waiting for transfers between devices, extended(): lax.ppermute(tail, axis, [(i, (i + 1) % count) for i in range(count)])  43.4 us
    gather x1, local copies, waits for them, and re-layouts, body(): picked = jnp.take(spread, local_ids, axis=0)  27.8 us
    unnamed x20, local copies, waits for them, and re-layouts  18.6 us
    reshape x1, local copies, waits for them, and re-layouts, body(): keyval = keyval.reshape(cells, count_nbr, 2 * width)  16.3 us
    concatenate x1, other arithmetic, extended(): jnp.concatenate([lax.ppermute(tail, axis, [(i, (i + 1) % count) for i in...  15.9 us
    all_to_all x1, waiting for transfers between devices, body(): lax.all_to_all(packed, 'dev', split_axis=0, concat_axis=0, tiled=True)  11.7 us
    dot_general x1, matrix products, body(): jnp.dot(picked, w_keyval, preferred_element_type=jnp.float32)  11.2 us
  transfers between devices with their start and end apart: 5, of which 4 were waited for; matrix products, arithmetic and copies ran while one was open for 3% of the time, Pallas kernels for 0%

commit v1 on v0

v1 whole, which is shorter than its diff:
```python
import jax
import jax.numpy as jnp
from jax import lax
from jax.experimental import pallas as pl
from jax.experimental.pallas import tpu as pltpu
from jax.sharding import PartitionSpec as P

MESH = pl.DeviceIdType.MESH
F32, BF16, I32 = jnp.float32, jnp.bfloat16, jnp.int32

HEADS = 8
HEAD = 64
NBR = 20
CELLS = 256
WIDTH = 512
EVENTS = 512
CAP = 96
HALF = CAP // 2
PACK = CAP + HALF
FEAT = 172
TAIL = FEAT - 128
ROWS = 112
LANES = 128
ROLES = 3
OWNERS = 16
SIDE = 4
RANGES = 16
BUCKETS = OWNERS * ROLES
LAG = 2

ORDER = (
    (0, 0), (0, 3), (0, 1), (3, 0), (1, 0), (3, 3), (1, 1), (0, 2),
    (2, 0), (3, 1), (1, 3), (3, 2), (1, 2), (2, 3), (2, 1), (2, 2),
)
SLOT = {rel: slot for slot, rel in enumerate(ORDER)}


def gather_plan():
    names, messages = {}, []

    def add(name, source, hop, first, rows):
        target = ((source[0] - hop[0]) % SIDE, (source[1] - hop[1]) % SIDE)
        names[name] = len(messages)
        messages.append((SLOT[source], SLOT[target], first, rows, hop))

    for cls in "ab":
        base = 0 if cls == "a" else 128

        def at(first, second, cls=cls):
            return (second % SIDE, first % SIDE) if cls == "a" else (first % SIDE, second % SIDE)

        for sign in (1, -1):
            add((cls, 1, 0, sign), at(0, 0), at(sign, 0), base, 128)
            add((cls, 2, 0, sign), at(-sign, 0), at(sign, 0), base + (0 if sign > 0 else 64), 64)
            for off in (0, -1, 1, 2):
                add((cls, 3, off, sign), at(off, 0), at(0, sign), base, 128)
                first = base + (0 if sign > 0 else 64)
                add((cls, 4, off, sign), at(off, -sign), at(0, sign), first, 64)

    def both(*items):
        return [names[(cls,) + item] for item in items for cls in "ab"]

    start = both((1, 0, 1), (1, 0, -1), (3, 0, 1), (3, 0, -1))
    steps = {
        1: [
            (
                both((1, 0, 1), (1, 0, -1)),
                both((2, 0, 1), (2, 0, -1), (3, -1, 1), (3, 1, -1)),
            ),
            (
                both((3, 0, 1), (3, 0, -1)),
                both((4, 0, 1), (4, 0, -1), (3, 1, 1), (3, -1, -1)),
            ),
        ],
        3: [(both((2, 0, 1), (2, 0, -1)), both((3, 2, 1), (3, 2, -1)))],
        5: [(both((3, -1, 1)), both((4, -1, 1)))],
        6: [(both((3, 1, -1)), both((4, 1, -1)))],
        7: [([names[("b", 4, 0, 1)], names[("b", 4, 0, -1)]], [])],
        8: [([names[("a", 4, 0, 1)], names[("a", 4, 0, -1)]], [])],
        9: [
            (
                [names[("a", 3, 1, 1)], names[("b", 3, -1, -1)]],
                [names[("a", 4, 1, 1)], names[("b", 4, -1, -1)]],
            )
        ],
        10: [
            (
                [names[("a", 3, -1, -1)], names[("b", 3, 1, 1)]],
                [names[("a", 4, -1, -1)], names[("b", 4, 1, 1)]],
            )
        ],
        11: [
            (both((3, 2, 1), (3, 2, -1)), both((4, 2, 1), (4, 2, -1))),
            ([names[("b", 4, -1, 1)], names[("b", 4, -1, -1)]], []),
        ],
        12: [([names[("b", 4, 1, 1)], names[("b", 4, 1, -1)]], [])],
        13: [([names[("a", 4, -1, 1)], names[("a", 4, -1, -1)]], [])],
        14: [([names[("a", 4, 1, 1)], names[("a", 4, 1, -1)]], [])],
        15: [(both((4, 2, 1), (4, 2, -1)), [])],
    }
    return messages, start, steps


MESSAGES, START, STEPS = gather_plan()
COUNT = len(MESSAGES)


def iota(shape, dim):
    return lax.broadcasted_iota(I32, shape, dim)


def dot(a, b):
    return jnp.dot(a, b, preferred_element_type=F32)


def dot_nt(a, b):
    return lax.dot_general(a, b, (((1,), (1,)), ((), ())), preferred_element_type=F32)


def dot_tn(a, b):
    return lax.dot_general(a, b, (((0,), (0,)), ((), ())), preferred_element_type=F32)


def ones_where(mask):
    return jnp.where(mask, 1.0, 0.0).astype(BF16)


def sigmoid(x):
    return 0.5 * jnp.tanh(0.5 * x) + 0.5


def kernel(
    mem_ref, feat_ref, dest_ref, slot_ref, nbr_ref, wmsg_ref,
    win_hbm, whid_hbm, wq_hbm, wkv_hbm, wout_hbm,
    new_ref, emb_ref,
    win, whid, wq, wkv, wout,
    tail, wtail, ev_out, ev_in, gh, sums, cnt,
    bkt, ind, tabs, reqs, celltab, cmat,
    blocks, picks, to_left, to_right, q_ref, vals, scores, probs, spread,
    w_sem, ev_send, ev_recv, rq_send, rq_recv, bl_send, bl_recv, pk_send, pk_recv,
):
    group, dev = lax.axis_index("group"), lax.axis_index("dev")
    y, x = dev // SIDE, dev % SIDE
    left, right = (group + RANGES - 1) % RANGES, (group + 1) % RANGES

    def owner(dy, dx):
        return ((y + dy) % SIDE) * SIDE + (x + dx) % SIDE

    barrier = pltpu.get_barrier_semaphore()

    def greet(k, _):
        pl.semaphore_signal(
            barrier, inc=1, device_id=(group, owner(k // SIDE, k % SIDE)), device_id_type=MESH
        )
        return 0

    lax.fori_loop(1, OWNERS, greet, 0)
    for side in (left, right):
        pl.semaphore_signal(barrier, inc=1, device_id=(side, dev), device_id_type=MESH)

    loads = [
        pltpu.make_async_copy(src, dst, w_sem.at[i])
        for i, (src, dst) in enumerate(
            ((whid_hbm, whid), (win_hbm, win), (wq_hbm, wq), (wkv_hbm, wkv), (wout_hbm, wout))
        )
    ]
    for load in loads:
        load.start()

    tail[...] = jnp.zeros_like(tail)
    tail[0:TAIL, :] = feat_ref[128:FEAT, :].astype(F32)
    tail[TAIL : TAIL + 1, :] = (slot_ref[...] + 1).astype(F32)
    tails = tail[...].astype(BF16)
    blank = jnp.zeros((64, EVENTS), BF16)
    tails_lo = jnp.concatenate([tails, blank], axis=0)
    tails_hi = jnp.concatenate([blank, tails], axis=0)
    head = feat_ref[0:128, :]
    dest = dest_ref[...]
    mine = iota((OWNERS, EVENTS), 0) == dest
    upper = ones_where(iota((EVENTS, EVENTS), 0) < iota((EVENTS, EVENTS), 1))
    before = dot(ones_where(mine), upper)
    place = jnp.sum(jnp.where(mine, before, 0.0), axis=0, keepdims=True).astype(I32) + dest * CAP

    pl.semaphore_wait(barrier, OWNERS - 1 + 2)

    def ev_copy(k):
        return pltpu.make_async_remote_copy(
            src_ref=ev_out.at[k],
            dst_ref=ev_in.at[k],
            send_sem=ev_send.at[k],
            recv_sem=ev_recv.at[k],
            device_id=(group, owner(k // SIDE, k % SIDE)),
            device_id_type=MESH,
        )

    def pack(i, _):
        k = OWNERS - 1 - i
        pick = ones_where(iota((CAP, EVENTS), 0) == place - owner(k // SIDE, k % SIDE) * CAP)
        ev_out[k, 0:CAP, :] = dot_nt(pick, head).astype(BF16)
        ev_out[k, CAP:PACK, :] = (
            dot_nt(pick[0:HALF], tails_lo) + dot_nt(pick[HALF:CAP], tails_hi)
        ).astype(BF16)

        @pl.when(k > 0)
        def _():
            ev_copy(k).start()

        return 0

    lax.fori_loop(0, OWNERS, pack, 0)
    ev_in[0] = ev_out[0]

    ids = nbr_ref[...]
    role = ((ids >> 12) - group + 1 + RANGES) % RANGES
    named = (ids >> 8) & 15
    rel = (((named >> 2) - y) & 3) * SIDE + ((named - x) & 3)
    slot_of = jnp.zeros_like(rel)
    for number, (dy, dx) in enumerate(ORDER):
        slot_of = jnp.where(rel == dy * SIDE + dx, number, slot_of)
    bucket = slot_of * ROLES + role
    bkt[...] = bucket
    wanted = (ids & 255) + 1
    cell = iota((1, CELLS), 1) + 1
    ahead = ones_where(iota((CELLS, CELLS), 0) < iota((CELLS, CELLS), 1))
    offset = jnp.zeros((BUCKETS, 1), F32)
    bucket_ids, place_ids = iota((BUCKETS, CELLS), 0), iota((LANES, CELLS), 0)
    table = jnp.zeros((LANES, LANES), F32)
    cells_of = jnp.zeros((BUCKETS, LANES), F32)
    for j in range(NBR):
        inside = bucket_ids == bucket[j : j + 1, :]
        rank = dot(ones_where(inside), ahead) + offset
        offset = offset + jnp.sum(jnp.where(inside, 1.0, 0.0), axis=1, keepdims=True)
        rank = jnp.sum(jnp.where(inside, rank, 0.0), axis=0, keepdims=True).astype(I32)
        hot = ones_where(place_ids == rank)
        ind[0:LANES, j * CELLS : (j + 1) * CELLS] = hot
        ind[LANES : 2 * LANES, j * CELLS : (j + 1) * CELLS] = hot
        asked = jnp.where(inside, wanted[j : j + 1, :].astype(F32), 0.0).astype(BF16)
        by = jnp.where(inside, cell.astype(F32), 0.0).astype(BF16)
        both = jnp.concatenate([asked, by, jnp.zeros((LANES - 2 * BUCKETS, CELLS), BF16)], axis=0)
        table = table + dot_nt(hot, both)
        cells_of = cells_of + dot_nt(by, hot)
    tabs[...] = table.astype(BF16)
    celltab[...] = cells_of

    asks = [
        pltpu.make_async_remote_copy(
            src_ref=tabs,
            dst_ref=reqs.at[i],
            send_sem=rq_send.at[i],
            recv_sem=rq_recv.at[i],
            device_id=(side, dev),
            device_id_type=MESH,
        )
        for i, side in enumerate((right, left))
    ]
    for ask in asks:
        ask.start()

    loads[0].wait()
    memory = mem_ref[...]
    for part in range(3):
        columns = slice(part * WIDTH, (part + 1) * WIDTH)
        gh[:, columns] = dot(memory, whid[:, columns])

    def cell_matrix(s, _):
        for r in range(ROLES):
            row = celltab[pl.ds(s * ROLES + r, 1), :]
            hot = ones_where((iota((CELLS, LANES), 0) + 1).astype(F32) == row)
            cmat[s, :, r * LANES : (r + 1) * LANES] = hot
            vals[s, r * LANES + ROWS : (r + 1) * LANES, :] = jnp.zeros((LANES - ROWS, WIDTH), BF16)
        return 0

    lax.fori_loop(0, OWNERS, cell_matrix, 0)
    scores[...] = jnp.zeros_like(scores)
    wtail[...] = jnp.zeros_like(wtail)
    wtail[0:TAIL, :] = wmsg_ref[128:FEAT, :].astype(F32)
    w_tail = wtail[...].astype(BF16)
    w_blank = jnp.zeros((64, WIDTH), BF16)
    w_lo = jnp.concatenate([wmsg_ref[0:128, :], w_tail, w_blank], axis=0)
    w_hi = jnp.concatenate([wmsg_ref[0:128, :], w_blank, w_tail], axis=0)

    sums[...] = jnp.zeros_like(sums)
    cnt[...] = jnp.zeros_like(cnt)
    for chunk in (1, 0):
        first = chunk * 8

        def arrived(k, _):
            ev_copy(k).wait_recv()
            return 0

        lax.fori_loop(max(first, 1), first + 8, arrived, 0)
        tail_in = ev_in[first : first + 8, CAP:PACK, :].reshape(8 * HALF, 128)
        for part, weights in enumerate((w_lo, w_hi)):
            main = ev_in[first : first + 8, part * HALF : (part + 1) * HALF, :].reshape(
                8 * HALF, 128
            )
            raw = dot(jnp.concatenate([main, tail_in], axis=1), weights)
            message = (raw * sigmoid(raw)).astype(BF16)
            column = ones_where(iota((16, 128), 1) == 64 * part + TAIL)
            marks = dot_nt(column, tail_in)[0:1, :]
            here = (iota((CELLS, 8 * HALF), 0) + 1).astype(F32) == marks
            sums[...] += dot(ones_where(here), message)
            cnt[...] += jnp.sum(jnp.where(here, 1.0, 0.0), axis=1, keepdims=True)

    counts = cnt[:, 0:1]
    mean_msg = (sums[...] / jnp.maximum(counts, 1.0)).astype(BF16)
    loads[1].wait()
    gate_z = sigmoid(dot(mean_msg, win[:, 0:WIDTH]) + gh[:, 0:WIDTH])
    gate_r = sigmoid(dot(mean_msg, win[:, WIDTH : 2 * WIDTH]) + gh[:, WIDTH : 2 * WIDTH])
    cand = jnp.tanh(dot(mean_msg, win[:, 2 * WIDTH :]) + gate_r * gh[:, 2 * WIDTH :])
    old = memory.astype(F32)
    updated = (1.0 - gate_z) * old + gate_z * cand
    new_memory = jnp.where(counts > 0, updated, old).astype(BF16)
    blocks[0] = new_memory
    new_ref[...] = new_memory

    def bl_copy(number):
        source, target, first, rows, (dy, dx) = MESSAGES[number]
        return pltpu.make_async_remote_copy(
            src_ref=blocks.at[source, pl.ds(first, rows)],
            dst_ref=blocks.at[target, pl.ds(first, rows)],
            send_sem=bl_send.at[number],
            recv_sem=bl_recv.at[number],
            device_id=(group, owner(dy, dx)),
            device_id_type=MESH,
        )

    def pk_copy(side, s):
        source, first, target = ((to_right, 0, right), (to_left, 2 * ROWS, left))[side]
        return pltpu.make_async_remote_copy(
            src_ref=source.at[s],
            dst_ref=picks.at[s, pl.ds(first, ROWS)],
            send_sem=pk_send.at[side, s],
            recv_sem=pk_recv.at[side, s],
            device_id=(target, dev),
            device_id_type=MESH,
        )

    for number in START:
        bl_copy(number).start()
    loads[2].wait()
    q_ref[...] = (dot(new_memory, wq[...]) * (HEAD**-0.5)).astype(BF16)
    for ask in asks:
        ask.wait_recv()
    loads[3].wait()

    def chosen(tab, column):
        select = ones_where(iota((LANES, CELLS), 0) == column)
        values = dot(tab, select)
        return ones_where(values == (iota((ROWS, CELLS), 1) + 1).astype(F32))

    head_rows = ones_where(iota((16, WIDTH), 0) == iota((16, WIDTH), 1) // HEAD)

    def step(s, _):
        @pl.when(s < OWNERS)
        def _():
            for at, stages in STEPS.items():

                @pl.when(s == at)
                def _(stages=stages):
                    for awaited, sent in stages:
                        for number in awaited:
                            bl_copy(number).wait_recv()
                        for number in sent:
                            bl_copy(number).start()

            block = blocks[s]
            for_right = chosen(reqs[1, 0:ROWS, :], s * ROLES)
            for_left = chosen(reqs[0, 0:ROWS, :], s * ROLES + 2)
            for_own = chosen(tabs[0:ROWS, :], s * ROLES + 1)
            got = dot(jnp.concatenate([for_right, for_left, for_own], axis=0), block).astype(BF16)
            to_right[s] = got[0:ROWS]
            pk_copy(0, s).start()
            to_left[s] = got[ROWS : 2 * ROWS]
            pk_copy(1, s).start()
            picks[s, ROWS : 2 * ROWS, :] = got[2 * ROWS : 3 * ROWS]

        @pl.when(s >= LAG)
        def _():
            t = s - LAG
            for side in range(2):
                pk_copy(side, t).wait_recv()
            keyval = dot(picks[t], wkv[...])
            owned = jnp.concatenate(
                [
                    chosen(tabs[0:ROWS, :], BUCKETS + t * ROLES + r)
                    for r in range(ROLES)
                ],
                axis=0,
            )
            product = dot(owned, q_ref[...]) * keyval[:, 0:WIDTH].astype(BF16).astype(F32)
            upper_part = product.astype(BF16)
            lower_part = (product - upper_part.astype(F32)).astype(BF16)
            values = keyval[:, WIDTH:].astype(BF16)
            for r in range(ROLES):
                rows = slice(r * ROWS, (r + 1) * ROWS)
                score = dot_nt(head_rows, upper_part[rows]) + dot_nt(head_rows, lower_part[rows])
                first = pl.multiple_of((t * ROLES + r) * HEADS, HEADS)
                scores[pl.ds(first, HEADS), 0:ROWS] = score[0:HEADS]
                vals[t, r * LANES : r * LANES + ROWS, :] = values[rows]

        return 0

    lax.fori_loop(0, OWNERS + LAG, step, 0)

    all_scores = scores[...]
    upper_part = all_scores.astype(BF16)
    lower_part = (all_scores - upper_part.astype(F32)).astype(BF16)
    parts = jnp.concatenate([upper_part, lower_part], axis=1)
    numbers = lax.broadcasted_iota(I32, (BUCKETS, HEADS, CELLS), 0)
    for j in range(NBR):
        found = dot(parts, ind[:, j * CELLS : (j + 1) * CELLS]).reshape(BUCKETS, HEADS, CELLS)
        inside = numbers == bkt[j : j + 1, :].reshape(1, 1, CELLS)
        probs[j] = jnp.sum(jnp.where(inside, found, 0.0), axis=0)
    top = probs[0]
    for j in range(1, NBR):
        top = jnp.maximum(top, probs[j])
    total = jnp.zeros_like(top)
    for j in range(NBR):
        raised = jnp.exp(probs[j] - top)
        probs[j] = raised
        total = total + raised
    inverse = 1.0 / total
    for j in range(NBR):
        weight = (probs[j] * inverse).astype(BF16).astype(F32)
        inside = numbers == bkt[j : j + 1, :].reshape(1, 1, CELLS)
        placed = jnp.where(inside, weight[None], 0.0).reshape(BUCKETS * HEADS, CELLS)
        spread[:, j * CELLS : (j + 1) * CELLS] = placed.astype(BF16)
    scores[...] = dot_nt(spread[...], ind[0:LANES, :])

    sums[...] = jnp.zeros_like(sums)
    widen = ones_where(iota((HEADS, WIDTH), 0) == iota((HEADS, WIDTH), 1) // HEAD)

    def weigh(s, _):
        weighted = []
        for r in range(ROLES):
            first = pl.multiple_of((s * ROLES + r) * HEADS, HEADS)
            wide = dot_tn(scores[pl.ds(first, HEADS), :].astype(BF16), widen)
            value = vals[s, r * LANES : (r + 1) * LANES, :].astype(F32)
            weighted.append((wide * value).astype(BF16))
        sums[...] += dot(cmat[s], jnp.concatenate(weighted, axis=0))
        return 0

    lax.fori_loop(0, OWNERS, weigh, 0)
    attended = sums[...].astype(BF16)
    loads[4].wait()
    emb_ref[...] = (blocks[0].astype(F32) + dot(attended, wout[...])).astype(BF16)

    def sent(k, _):
        ev_copy(k).wait_send()
        return 0

    lax.fori_loop(1, OWNERS, sent, 0)
    for ask in asks:
        ask.wait_send()
    for number in range(COUNT):
        bl_copy(number).wait_send()

    def given(s, _):
        for side in range(2):
            pk_copy(side, s).wait_send()
        return 0

    lax.fori_loop(0, OWNERS, given, 0)


def body(memory, features, dest, slot, neighbours, w_message, w_input, w_hidden, w_query, w_keyval, w_output):
    inside = pl.BlockSpec(memory_space=pltpu.VMEM)
    outside = pl.BlockSpec(memory_space=pl.ANY)
    vmem, dma = pltpu.VMEM, pltpu.SemaphoreType.DMA
    return pl.pallas_call(
        kernel,
        out_shape=(
            jax.ShapeDtypeStruct((CELLS, WIDTH), BF16),
            jax.ShapeDtypeStruct((CELLS, WIDTH), BF16),
        ),
        in_specs=[inside] * 6 + [outside] * 5,
        out_specs=(inside, inside),
        scratch_shapes=[
            vmem((WIDTH, 3 * WIDTH), BF16),
            vmem((WIDTH, 3 * WIDTH), BF16),
            vmem((WIDTH, WIDTH), BF16),
            vmem((WIDTH, 2 * WIDTH), BF16),
            vmem((WIDTH, WIDTH), BF16),
            vmem((64, EVENTS), F32),
            vmem((64, WIDTH), F32),
            vmem((OWNERS, PACK, 128), BF16),
            vmem((OWNERS, PACK, 128), BF16),
            vmem((CELLS, 3 * WIDTH), F32),
            vmem((CELLS, WIDTH), F32),
            vmem((CELLS, LANES), F32),
            vmem((NBR, CELLS), I32),
            vmem((2 * LANES, NBR * CELLS), BF16),
            vmem((LANES, LANES), BF16),
            vmem((2, LANES, LANES), BF16),
            vmem((BUCKETS, LANES), F32),
            vmem((OWNERS, CELLS, ROLES * LANES), BF16),
            vmem((OWNERS, CELLS, WIDTH), BF16),
            vmem((OWNERS, ROLES * ROWS, WIDTH), BF16),
            vmem((OWNERS, ROWS, WIDTH), BF16),
            vmem((OWNERS, ROWS, WIDTH), BF16),
            vmem((CELLS, WIDTH), BF16),
            vmem((OWNERS, ROLES * LANES, WIDTH), BF16),
            vmem((BUCKETS * HEADS, LANES), F32),
            vmem((NBR, HEADS, CELLS), F32),
            vmem((BUCKETS * HEADS, NBR * CELLS), BF16),
            dma((5,)),
            dma((OWNERS,)),
            dma((OWNERS,)),
            dma((2,)),
            dma((2,)),
            dma((COUNT,)),
            dma((COUNT,)),
            dma((2, OWNERS)),
            dma((2, OWNERS)),
        ],
        compiler_params=pltpu.CompilerParams(
            collective_id=0, has_side_effects=True, vmem_limit_bytes=58 * 1024 * 1024
        ),
        cost_estimate=pl.CostEstimate(
            flops=12_000_000_000, bytes_accessed=6_000_000, transcendentals=2_000_000
        ),
    )(
        memory,
        features.T,
        dest.reshape(1, EVENTS),
        slot.reshape(1, EVENTS),
        neighbours.T,
        w_message,
        w_input,
        w_hidden,
        w_query,
        w_keyval,
        w_output,
    )


def solution(mesh):
    rows = P(("group", "dev"), None)
    placed = (rows, rows, rows, P(("group", "dev")), rows) + (P(),) * 6
    return jax.shard_map(
        body, mesh=mesh, in_specs=placed, out_specs=(rows, rows), check_vma=False
    )
```

time: 279 us -> 79.7 us (0.29)
  waiting for transfers between devices: 115 us -> 0 us
  local copies, waits for them, and re-layouts: 81.5 us -> 3.34 us
  Pallas kernels: 0 us -> 75.3 us
  other arithmetic: 29.9 us -> 0 us
  matrix products: 20.3 us -> 0 us
  starting transfers between devices: 16.5 us -> 0 us
  between operations: 14.3 us -> 0.64 us
    pallas_call x0 -> x1, Pallas kernels: none -> 75.3 us  [body(): pl.pallas_call(kernel, out_shape=(jax.ShapeDtypeStruct((CELLS, WIDTH), BF...]
    all_gather x1 -> x0, waiting for transfers between devices: 56.6 us -> none  [body(): block = lax.all_gather(new_memory, 'dev', axis=0, tiled=True)]
    ppermute x2 -> x0, waiting for transfers between devices: 47.1 us -> none  [the longest x1 43.4 us: extended(): lax.ppermute(tail, axis, [(i, (i + 1) % count) for i in range(count)])]
    gather x1 -> x0, local copies, waits for them, and re-layouts: 27.8 us -> none  [body(): picked = jnp.take(spread, local_ids, axis=0)]
    dot_general x6 -> x0, matrix products: 20.3 us -> none  [the longest x1 11.2 us: body(): jnp.dot(picked, w_keyval, preferred_element_type=jnp.float32)]
    reshape x5 -> x0, local copies, waits for them, and re-layouts: 18.6 us -> none  [the longest x1 16.3 us: body(): keyval = keyval.reshape(cells, count_nbr, 2 * width)]
    concatenate x1 -> x0, other arithmetic: 15.9 us -> none  [extended(): jnp.concatenate([lax.ppermute(tail, axis, [(i, (i + 1) % count) for i in...]
    unnamed x20 -> x2, local copies, waits for them, and re-layouts: 18.6 us -> 3.34 us
  transfers between devices with their start and end apart: 5 -> 0, of which waited for: 4 -> 0; matrix products, arithmetic and copies ran while one was open for 3% -> 0% of each run, Pallas kernels for 0% -> 0%
where the time goes in v1:
time: 79.7 us; the launch traced here: 79.3 us
  Pallas kernels  75.3 us (94%)
  local copies, waits for them, and re-layouts  3.34 us (4%)
    pallas_call x1, Pallas kernels, body(): pl.pallas_call(kernel, out_shape=(jax.ShapeDtypeStruct((CELLS, WIDTH), BF...  75.3 us
    unnamed x2, local copies, waits for them, and re-layouts  3.34 us

profile of v1, /device:TPU:97, one launch (start us, length us, event | category | flops | bytes accessed | tf_op | source)
XLA Modules:
  0.0 79.3 jit_solution(15006812349371330282)
XLA Ops:
  0.6 75.3 %shard_map.122 = (bf16[256,512]{1,0:T(8,128)(2,1)}, bf16[256,512]{1,0:T(8,128)(2,1)}) custom-call(bf16[256,512]{1,0:T(8,128)(2,1)} %mem_ref.1, bf16[172,512]{1,0:T(8,128)(2,1)} %bitcast.4, s32[1,512]{1,0:T(1,128)} %bitcast.6, s32[1,512]{1,0:T(1,128)} %bitcast.7, s32[20,256]{1,0:T(8,128)} %bitcast.5, bf16[172,512]{1,0:T(8,128)(2,1)} %wmsg_ref.1, ...), custom_call_target="tpu_custom_call" | custom-call | flops 12000000000 | bytes 6000000 | tf_op jit(solution)/shard_map/pallas_call | solution.py:471
  75.9 1.7 %copy.15 = bf16[256,512]{1,0:T(8,128)(2,1)} copy(bf16[256,512]{1,0:T(8,128)(2,1)} %get-tuple-element.4) | data formatting | bytes 524288
  77.6 1.7 %copy.16 = bf16[256,512]{1,0:T(8,128)(2,1)} copy(bf16[256,512]{1,0:T(8,128)(2,1)} %get-tuple-element.5) | data formatting | bytes 524288

commit v2 on v1

v2 whole, which is shorter than its diff:
```python
import jax
import jax.numpy as jnp
from jax import lax
from jax.experimental import pallas as pl
from jax.experimental.pallas import tpu as pltpu
from jax.sharding import PartitionSpec as P

MESH = pl.DeviceIdType.MESH
F32, BF16, I32 = jnp.float32, jnp.bfloat16, jnp.int32

HEADS = 8
HEAD = 64
NBR = 20
CELLS = 256
WIDTH = 512
EVENTS = 512
CAP = 96
HALF = CAP // 2
PACK = CAP + HALF
FEAT = 172
TAIL = FEAT - 128
ROWS = 112
LANES = 128
ROLES = 3
OWNERS = 16
SIDE = 4
RANGES = 16
BUCKETS = OWNERS * ROLES
TILE = 256
LAG = 5
BATCH = 4

ORDER = (
    (0, 0), (0, 3), (0, 1), (3, 0), (1, 0), (3, 3), (1, 1), (0, 2),
    (2, 0), (3, 1), (1, 3), (3, 2), (1, 2), (2, 3), (2, 1), (2, 2),
)
SLOT = {rel: slot for slot, rel in enumerate(ORDER)}


def gather_plan():
    names, messages = {}, []

    def add(name, source, hop, first, rows):
        target = ((source[0] - hop[0]) % SIDE, (source[1] - hop[1]) % SIDE)
        names[name] = len(messages)
        messages.append((SLOT[source], SLOT[target], first, rows, hop))

    for cls in "ab":
        base = 0 if cls == "a" else 128

        def at(first, second, cls=cls):
            return (second % SIDE, first % SIDE) if cls == "a" else (first % SIDE, second % SIDE)

        for sign in (1, -1):
            add((cls, 1, 0, sign), at(0, 0), at(sign, 0), base, 128)
            add((cls, 2, 0, sign), at(-sign, 0), at(sign, 0), base + (0 if sign > 0 else 64), 64)
            for off in (0, -1, 1, 2):
                add((cls, 3, off, sign), at(off, 0), at(0, sign), base, 128)
                first = base + (0 if sign > 0 else 64)
                add((cls, 4, off, sign), at(off, -sign), at(0, sign), first, 64)

    def both(*items):
        return [names[(cls,) + item] for item in items for cls in "ab"]

    start = both((1, 0, 1), (1, 0, -1), (3, 0, 1), (3, 0, -1))
    steps = {
        1: [
            (
                both((1, 0, 1), (1, 0, -1)),
                both((2, 0, 1), (2, 0, -1), (3, -1, 1), (3, 1, -1)),
            ),
            (
                both((3, 0, 1), (3, 0, -1)),
                both((4, 0, 1), (4, 0, -1), (3, 1, 1), (3, -1, -1)),
            ),
        ],
        3: [(both((2, 0, 1), (2, 0, -1)), both((3, 2, 1), (3, 2, -1)))],
        5: [(both((3, -1, 1)), both((4, -1, 1)))],
        6: [(both((3, 1, -1)), both((4, 1, -1)))],
        7: [([names[("b", 4, 0, 1)], names[("b", 4, 0, -1)]], [])],
        8: [([names[("a", 4, 0, 1)], names[("a", 4, 0, -1)]], [])],
        9: [
            (
                [names[("a", 3, 1, 1)], names[("b", 3, -1, -1)]],
                [names[("a", 4, 1, 1)], names[("b", 4, -1, -1)]],
            )
        ],
        10: [
            (
                [names[("a", 3, -1, -1)], names[("b", 3, 1, 1)]],
                [names[("a", 4, -1, -1)], names[("b", 4, 1, 1)]],
            )
        ],
        11: [
            (both((3, 2, 1), (3, 2, -1)), both((4, 2, 1), (4, 2, -1))),
            ([names[("b", 4, -1, 1)], names[("b", 4, -1, -1)]], []),
        ],
        12: [([names[("b", 4, 1, 1)], names[("b", 4, 1, -1)]], [])],
        13: [([names[("a", 4, -1, 1)], names[("a", 4, -1, -1)]], [])],
        14: [([names[("a", 4, 1, 1)], names[("a", 4, 1, -1)]], [])],
        15: [(both((4, 2, 1), (4, 2, -1)), [])],
    }
    return messages, start, steps


MESSAGES, START, STEPS = gather_plan()
COUNT = len(MESSAGES)
GROUPS = [awaited for stages in STEPS.values() for awaited, _ in stages]
GROUP_OF = {number: group for group, awaited in enumerate(GROUPS) for number in awaited}
SENT_BLOCKS = sum(message[3] for message in MESSAGES) // CELLS


def iota(shape, dim):
    return lax.broadcasted_iota(I32, shape, dim)


def dot(a, b):
    return jnp.dot(a, b, preferred_element_type=F32)


def dot_nt(a, b):
    return lax.dot_general(a, b, (((1,), (1,)), ((), ())), preferred_element_type=F32)


def dot_tn(a, b):
    return lax.dot_general(a, b, (((0,), (0,)), ((), ())), preferred_element_type=F32)


def ones_where(mask):
    return jnp.where(mask, 1.0, 0.0).astype(BF16)


def sigmoid(x):
    return 0.5 * jnp.tanh(0.5 * x) + 0.5


def kernel(
    mem_ref, feat_ref, dest_ref, slot_ref, nbr_ref, wmsg_ref,
    win_hbm, whid_hbm, wq_hbm, wkv_hbm, wout_hbm,
    new_ref, emb_ref,
    win, whid, wq, wkv, wout,
    tail, wtail, ev_out, ev_in, gh, sums, cnt,
    mean_msg, w_both, row_hot, cell_hot, bkt, wanted, table, ind, tabs, reqs, celltab, cmat,
    blocks, picks, to_left, to_right, q_ref, vals, scores, probs,
    w_sem, ev_send, ev_recv, rq_send, rq_recv, bl_send, bl_recv, pk_send, pk_recv,
):
    group, dev = lax.axis_index("group"), lax.axis_index("dev")
    y, x = dev // SIDE, dev % SIDE
    left, right = (group + RANGES - 1) % RANGES, (group + 1) % RANGES

    def owner(dy, dx):
        return ((y + dy) % SIDE) * SIDE + (x + dx) % SIDE

    def finish(part, sem):
        pltpu.make_async_copy(part, part, sem).wait()

    barrier = pltpu.get_barrier_semaphore()

    def greet(k, _):
        pl.semaphore_signal(
            barrier, inc=1, device_id=(group, owner(k // SIDE, k % SIDE)), device_id_type=MESH
        )
        return 0

    lax.fori_loop(1, OWNERS, greet, 0)
    for side in (left, right):
        pl.semaphore_signal(barrier, inc=1, device_id=(side, dev), device_id_type=MESH)

    loads = [
        pltpu.make_async_copy(src, dst, w_sem.at[i])
        for i, (src, dst) in enumerate(
            ((whid_hbm, whid), (win_hbm, win), (wq_hbm, wq), (wkv_hbm, wkv), (wout_hbm, wout))
        )
    ]
    for load in loads:
        load.start()

    tail[...] = jnp.zeros_like(tail)
    tail[0:TAIL, :] = feat_ref[128:FEAT, :].astype(F32)
    tail[TAIL : TAIL + 1, :] = (slot_ref[...] + 1).astype(F32)
    tails = tail[...].astype(BF16)
    blank = jnp.zeros((64, EVENTS), BF16)
    head = feat_ref[0:128, :]
    feats = (
        jnp.concatenate([head, tails, blank], axis=0),
        jnp.concatenate([head, blank, tails], axis=0),
    )
    dest = dest_ref[...]
    mine = iota((OWNERS, EVENTS), 0) == dest
    upper = ones_where(iota((EVENTS, EVENTS), 0) < iota((EVENTS, EVENTS), 1))
    before = dot(ones_where(mine), upper)
    place = jnp.sum(jnp.where(mine, before, 0.0), axis=0, keepdims=True).astype(I32) + dest * CAP

    def ev_copy(k):
        return pltpu.make_async_remote_copy(
            src_ref=ev_out.at[k],
            dst_ref=ev_in.at[k],
            send_sem=ev_send.at[0],
            recv_sem=ev_recv.at[k // 8],
            device_id=(group, owner(k // SIDE, k % SIDE)),
            device_id_type=MESH,
        )

    def pack(i, _):
        rows = SIDE - 1 - i
        packed = []
        for part in range(2):
            pick = [
                iota((HALF, EVENTS), 0) == place - (owner(rows, column) * CAP + part * HALF)
                for column in range(SIDE)
            ]
            pick = jnp.concatenate([ones_where(one) for one in pick], axis=0)
            packed.append(dot_nt(pick, feats[part]))
        for column in range(SIDE):
            k = rows * SIDE + column
            at = slice(column * HALF, (column + 1) * HALF)
            ev_out[k, 0:HALF, :] = packed[0][at, 0:128].astype(BF16)
            ev_out[k, HALF:CAP, :] = packed[1][at, 0:128].astype(BF16)
            ev_out[k, CAP:PACK, :] = (packed[0][at, 128:] + packed[1][at, 128:]).astype(BF16)
        return 0

    lax.fori_loop(0, SIDE, pack, 0)
    ev_in[0] = ev_out[0]
    pl.semaphore_wait(barrier, OWNERS - 1 + 2)

    def send_events(i, _):
        ev_copy(OWNERS - 1 - i).start()
        return 0

    lax.fori_loop(0, OWNERS - 1, send_events, 0)

    ids = nbr_ref[...]
    role = ((ids >> 12) - group + 1 + RANGES) % RANGES
    named = (ids >> 8) & 15
    rel = (((named >> 2) - y) & 3) * SIDE + ((named - x) & 3)
    slot_of = jnp.zeros_like(rel)
    for number, (dy, dx) in enumerate(ORDER):
        slot_of = jnp.where(rel == dy * SIDE + dx, number, slot_of)
    bucket = slot_of * ROLES + role
    bkt[...] = bucket
    wanted[...] = (ids & 255) + 1
    ahead = ones_where(iota((CELLS, CELLS), 0) < iota((CELLS, CELLS), 1))
    bucket_ids, place_ids = iota((BUCKETS, CELLS), 0), iota((LANES, CELLS), 0)
    cell = jnp.broadcast_to((iota((1, CELLS), 1) + 1).astype(F32), (BUCKETS, CELLS))
    filler = jnp.zeros((LANES - 2 * BUCKETS, CELLS), BF16)
    table[...] = jnp.zeros_like(table)

    def tabulate(i, offset):
        inside = [bucket_ids == bkt[pl.ds(i * BATCH + j, 1), :] for j in range(BATCH)]
        before = dot(jnp.concatenate([ones_where(one) for one in inside], axis=0), ahead)
        hots, boths = [], []
        for j in range(BATCH):
            rank = before[j * BUCKETS : (j + 1) * BUCKETS] + offset
            offset = offset + jnp.sum(jnp.where(inside[j], 1.0, 0.0), axis=1, keepdims=True)
            rank = jnp.sum(jnp.where(inside[j], rank, 0.0), axis=0, keepdims=True).astype(I32)
            hot = ones_where(place_ids == rank)
            at = pl.ds(pl.multiple_of((i * BATCH + j) * CELLS, CELLS), CELLS)
            ind[0:LANES, at] = hot
            ind[LANES : 2 * LANES, at] = hot
            row = wanted[pl.ds(i * BATCH + j, 1), :].astype(F32)
            asked = jnp.where(inside[j], row, 0.0).astype(BF16)
            by = jnp.where(inside[j], cell, 0.0).astype(BF16)
            hots.append(hot)
            boths.append(jnp.concatenate([asked, by, filler], axis=0))
        table[...] += dot_nt(jnp.concatenate(hots, axis=1), jnp.concatenate(boths, axis=1))
        return offset

    lax.fori_loop(0, NBR // BATCH, tabulate, jnp.zeros((BUCKETS, 1), F32))
    tabs[...] = table[...].astype(BF16)
    celltab[...] = table[...].T[BUCKETS : 2 * BUCKETS, :]

    asks = [
        pltpu.make_async_remote_copy(
            src_ref=tabs,
            dst_ref=reqs.at[i],
            send_sem=rq_send.at[i],
            recv_sem=rq_recv.at[i],
            device_id=(side, dev),
            device_id_type=MESH,
        )
        for i, side in enumerate((right, left))
    ]
    for ask in asks:
        ask.start()

    def chosen(tab, column):
        select = ones_where(iota((LANES, CELLS), 0) == column)
        values = dot(tab[0:ROWS, :], select)
        return ones_where(values == (iota((ROWS, CELLS), 1) + 1).astype(F32))

    def cell_matrix(s, _):
        for r in range(ROLES):
            row = celltab[pl.ds(s * ROLES + r, 1), :]
            hot = ones_where((iota((CELLS, LANES), 0) + 1).astype(F32) == row)
            cmat[s, :, r * LANES : (r + 1) * LANES] = hot
            cell_hot[s, r * ROWS : (r + 1) * ROWS, :] = chosen(tabs, BUCKETS + s * ROLES + r)
            vals[s, r * LANES + ROWS : (r + 1) * LANES, :] = jnp.zeros((LANES - ROWS, WIDTH), BF16)
        row_hot[s, 2 * ROWS : 3 * ROWS, :] = chosen(tabs, s * ROLES + 1)
        return 0

    lax.fori_loop(0, OWNERS, cell_matrix, 0)
    scores[...] = jnp.zeros_like(scores)
    loads[0].wait()

    def hidden(part, _):
        columns = pl.ds(pl.multiple_of(part * WIDTH, WIDTH), WIDTH)
        gh[:, columns] = dot(mem_ref[...], whid[:, columns])
        return 0

    lax.fori_loop(0, 3, hidden, 0)

    wtail[...] = jnp.zeros_like(wtail)
    wtail[0:TAIL, :] = wmsg_ref[128:FEAT, :].astype(F32)
    w_tail = wtail[...].astype(BF16)
    w_blank = jnp.zeros((64, WIDTH), BF16)
    w_both[0] = jnp.concatenate([wmsg_ref[0:128, :], w_tail, w_blank], axis=0)
    w_both[1] = jnp.concatenate([wmsg_ref[0:128, :], w_blank, w_tail], axis=0)

    sums[...] = jnp.zeros_like(sums)
    cnt[...] = jnp.zeros_like(cnt)

    def collect(i, _):
        first = (1 - i) * 8

        @pl.when(i == 0)
        def _():
            finish(ev_in.at[pl.ds(8, 8)], ev_recv.at[1])

        @pl.when(i == 1)
        def _():
            finish(ev_in.at[pl.ds(1, 7)], ev_recv.at[0])

        tail_in = ev_in[pl.ds(first, 8), CAP:PACK, :].reshape(8 * HALF, 128)
        for part in range(2):
            main = ev_in[pl.ds(first, 8), part * HALF : (part + 1) * HALF, :]
            main = main.reshape(8 * HALF, 128)
            raw = dot(jnp.concatenate([main, tail_in], axis=1), w_both[part])
            message = (raw * sigmoid(raw)).astype(BF16)
            column = ones_where(iota((16, 128), 1) == 64 * part + TAIL)
            marks = dot_nt(column, tail_in)[0:1, :]
            here = (iota((CELLS, 8 * HALF), 0) + 1).astype(F32) == marks
            sums[...] += dot(ones_where(here), message)
            cnt[...] += jnp.sum(jnp.where(here, 1.0, 0.0), axis=1, keepdims=True)
        return 0

    lax.fori_loop(0, 2, collect, 0)
    mean_msg[...] = (sums[...] / jnp.maximum(cnt[:, 0:1], 1.0)).astype(BF16)
    loads[1].wait()

    def update(tile, _):
        def columns(gate):
            return pl.ds(pl.multiple_of(gate * WIDTH + tile * TILE, TILE), TILE)

        mean = mean_msg[...]
        gate_z = sigmoid(dot(mean, win[:, columns(0)]) + gh[:, columns(0)])
        gate_r = sigmoid(dot(mean, win[:, columns(1)]) + gh[:, columns(1)])
        cand = jnp.tanh(dot(mean, win[:, columns(2)]) + gate_r * gh[:, columns(2)])
        old = mem_ref[:, columns(0)].astype(F32)
        updated = (1.0 - gate_z) * old + gate_z * cand
        new_memory = jnp.where(cnt[:, 0:1] > 0, updated, old).astype(BF16)
        blocks[0, :, columns(0)] = new_memory
        new_ref[:, columns(0)] = new_memory
        return 0

    lax.fori_loop(0, WIDTH // TILE, update, 0)

    def bl_copy(number):
        source, target, first, rows, (dy, dx) = MESSAGES[number]
        return pltpu.make_async_remote_copy(
            src_ref=blocks.at[source, pl.ds(first, rows)],
            dst_ref=blocks.at[target, pl.ds(first, rows)],
            send_sem=bl_send.at[0],
            recv_sem=bl_recv.at[GROUP_OF[number]],
            device_id=(group, owner(dy, dx)),
            device_id_type=MESH,
        )

    def pk_copy(side, s):
        source, first, target = ((to_right, 0, right), (to_left, 2 * ROWS, left))[side]
        return pltpu.make_async_remote_copy(
            src_ref=source.at[s],
            dst_ref=picks.at[s, pl.ds(first, ROWS)],
            send_sem=pk_send.at[side],
            recv_sem=pk_recv.at[s // 2],
            device_id=(target, dev),
            device_id_type=MESH,
        )

    def arrived(awaited):
        rows = sum(MESSAGES[number][3] for number in awaited)
        if rows > CELLS:
            part = blocks.at[pl.ds(0, rows // CELLS)]
        else:
            part = blocks.at[0, pl.ds(0, rows)]
        finish(part, bl_recv.at[GROUP_OF[awaited[0]]])

    for number in START:
        bl_copy(number).start()
    loads[2].wait()
    q_ref[...] = (dot(blocks[0], wq[...]) * (HEAD**-0.5)).astype(BF16)

    for ask in asks:
        ask.wait_recv()

    def requested(s, _):
        row_hot[s, 0:ROWS, :] = chosen(reqs.at[1], s * ROLES)
        row_hot[s, ROWS : 2 * ROWS, :] = chosen(reqs.at[0], s * ROLES + 2)
        return 0

    lax.fori_loop(0, OWNERS, requested, 0)
    loads[3].wait()

    head_rows = ones_where(iota((16, WIDTH), 0) == iota((16, WIDTH), 1) // HEAD)

    def step(s, _):
        @pl.when(s < OWNERS)
        def _():
            for at, stages in STEPS.items():

                @pl.when(s == at)
                def _(stages=stages):
                    for awaited, sent in stages:
                        arrived(awaited)
                        for number in sent:
                            bl_copy(number).start()

            got = dot(row_hot[s], blocks[s]).astype(BF16)
            to_right[s] = got[0:ROWS]
            pk_copy(0, s).start()
            to_left[s] = got[ROWS : 2 * ROWS]
            pk_copy(1, s).start()
            picks[s, ROWS : 2 * ROWS, :] = got[2 * ROWS : 3 * ROWS]

        @pl.when(jnp.logical_and(s >= LAG, s % 2 == 1))
        def _():
            t = s - LAG
            finish(to_left.at[pl.ds(0, 4)], pk_recv.at[t // 2])
            picked = picks[pl.ds(t, 2)].reshape(2 * ROLES * ROWS, WIDTH)
            keys = dot(picked, wkv[:, 0:WIDTH]).astype(BF16).astype(F32)
            owned = cell_hot[pl.ds(t, 2)].reshape(2 * ROLES * ROWS, CELLS)
            product = dot(owned, q_ref[...]) * keys
            upper_part = product.astype(BF16)
            lower_part = (product - upper_part.astype(F32)).astype(BF16)
            for r in range(2 * ROLES):
                rows = slice(r * ROWS, (r + 1) * ROWS)
                score = dot_nt(head_rows, upper_part[rows]) + dot_nt(head_rows, lower_part[rows])
                first = pl.multiple_of((t * ROLES + r) * HEADS, HEADS)
                scores[pl.ds(first, HEADS), 0:ROWS] = score[0:HEADS]
            values = dot(picked, wkv[:, WIDTH:]).astype(BF16)
            for r in range(2 * ROLES):
                vals[t + r // ROLES, (r % ROLES) * LANES : (r % ROLES) * LANES + ROWS, :] = values[
                    r * ROWS : (r + 1) * ROWS
                ]

        return 0

    lax.fori_loop(0, OWNERS + LAG - 1, step, 0)

    all_scores = scores[...]
    upper_part = all_scores.astype(BF16)
    lower_part = (all_scores - upper_part.astype(F32)).astype(BF16)
    parts = jnp.concatenate([upper_part, lower_part], axis=1)
    numbers = lax.broadcasted_iota(I32, (BUCKETS, HEADS, CELLS), 0)

    def entries(j):
        return pl.ds(pl.multiple_of(j * CELLS, CELLS), CELLS)

    def order_by_cell(i, top):
        for j in range(BATCH):
            j = i * BATCH + j
            found = dot(parts, ind[:, entries(j)]).reshape(BUCKETS, HEADS, CELLS)
            inside = numbers == bkt[pl.ds(j, 1), :].reshape(1, 1, CELLS)
            mine = jnp.sum(jnp.where(inside, found, 0.0), axis=0)
            probs[j] = mine
            top = jnp.maximum(top, mine)
        return top

    lowest = jnp.full((HEADS, CELLS), -jnp.inf, F32)
    top = lax.fori_loop(0, NBR // BATCH, order_by_cell, lowest)
    raised = jnp.exp(probs[...] - top[None])
    probs[...] = (raised * (1.0 / jnp.sum(raised, axis=0))[None]).astype(BF16).astype(F32)
    scores[...] = jnp.zeros_like(scores)

    def order_by_bucket(i, _):
        placed = []
        for j in range(BATCH):
            j = i * BATCH + j
            inside = numbers == bkt[pl.ds(j, 1), :].reshape(1, 1, CELLS)
            one = jnp.where(inside, probs[j][None], 0.0).reshape(BUCKETS * HEADS, CELLS)
            placed.append(one.astype(BF16))
        part = pl.ds(pl.multiple_of(i * BATCH * CELLS, BATCH * CELLS), BATCH * CELLS)
        scores[...] += dot_nt(jnp.concatenate(placed, axis=1), ind[0:LANES, part])
        return 0

    lax.fori_loop(0, NBR // BATCH, order_by_bucket, 0)

    sums[...] = jnp.zeros_like(sums)
    widen = ones_where(iota((HEADS, WIDTH), 0) == iota((HEADS, WIDTH), 1) // HEAD)

    def weigh(i, _):
        weighted = []
        for r in range(2 * ROLES):
            first = pl.multiple_of((2 * i * ROLES + r) * HEADS, HEADS)
            wide = dot_tn(scores[pl.ds(first, HEADS), :].astype(BF16), widen)
            value = vals[2 * i + r // ROLES, (r % ROLES) * LANES : (r % ROLES + 1) * LANES, :]
            weighted.append((wide * value.astype(F32)).astype(BF16))
        cells = jnp.concatenate([cmat[2 * i], cmat[2 * i + 1]], axis=1)
        sums[...] += dot(cells, jnp.concatenate(weighted, axis=0))
        return 0

    lax.fori_loop(0, OWNERS // 2, weigh, 0)
    attended = sums[...].astype(BF16)
    loads[4].wait()
    emb_ref[...] = (blocks[0].astype(F32) + dot(attended, wout[...])).astype(BF16)

    finish(ev_out.at[pl.ds(1, OWNERS - 1)], ev_send.at[0])
    for ask in asks:
        ask.wait_send()
    finish(blocks.at[pl.ds(0, SENT_BLOCKS)], bl_send.at[0])
    finish(to_right, pk_send.at[0])
    finish(to_left, pk_send.at[1])


def body(memory, features, dest, slot, neighbours, w_message, w_input, w_hidden, w_query, w_keyval, w_output):
    inside = pl.BlockSpec(memory_space=pltpu.VMEM)
    outside = pl.BlockSpec(memory_space=pl.ANY)
    vmem, dma = pltpu.VMEM, pltpu.SemaphoreType.DMA
    return pl.pallas_call(
        kernel,
        out_shape=(
            jax.ShapeDtypeStruct((CELLS, WIDTH), BF16),
            jax.ShapeDtypeStruct((CELLS, WIDTH), BF16),
        ),
        in_specs=[inside] * 6 + [outside] * 5,
        out_specs=(inside, inside),
        scratch_shapes=[
            vmem((WIDTH, 3 * WIDTH), BF16),
            vmem((WIDTH, 3 * WIDTH), BF16),
            vmem((WIDTH, WIDTH), BF16),
            vmem((WIDTH, 2 * WIDTH), BF16),
            vmem((WIDTH, WIDTH), BF16),
            vmem((64, EVENTS), F32),
            vmem((64, WIDTH), F32),
            vmem((OWNERS, PACK, 128), BF16),
            vmem((OWNERS, PACK, 128), BF16),
            vmem((CELLS, 3 * WIDTH), F32),
            vmem((CELLS, WIDTH), F32),
            vmem((CELLS, LANES), F32),
            vmem((CELLS, WIDTH), BF16),
            vmem((2, 256, WIDTH), BF16),
            vmem((OWNERS, ROLES * ROWS, CELLS), BF16),
            vmem((OWNERS, ROLES * ROWS, CELLS), BF16),
            vmem((NBR, CELLS), I32),
            vmem((NBR, CELLS), I32),
            vmem((LANES, LANES), F32),
            vmem((2 * LANES, NBR * CELLS), BF16),
            vmem((LANES, LANES), BF16),
            vmem((2, LANES, LANES), BF16),
            vmem((BUCKETS, LANES), F32),
            vmem((OWNERS, CELLS, ROLES * LANES), BF16),
            vmem((OWNERS, CELLS, WIDTH), BF16),
            vmem((OWNERS, ROLES * ROWS, WIDTH), BF16),
            vmem((OWNERS, ROWS, WIDTH), BF16),
            vmem((OWNERS, ROWS, WIDTH), BF16),
            vmem((CELLS, WIDTH), BF16),
            vmem((OWNERS, ROLES * LANES, WIDTH), BF16),
            vmem((BUCKETS * HEADS, LANES), F32),
            vmem((NBR, HEADS, CELLS), F32),
            dma((5,)),
            dma((1,)),
            dma((2,)),
            dma((2,)),
            dma((2,)),
            dma((1,)),
            dma((len(GROUPS),)),
            dma((2,)),
            dma((OWNERS // 2,)),
        ],
        compiler_params=pltpu.CompilerParams(
            collective_id=0, has_side_effects=True, vmem_limit_bytes=58 * 1024 * 1024
        ),
        cost_estimate=pl.CostEstimate(
            flops=12_000_000_000, bytes_accessed=6_000_000, transcendentals=2_000_000
        ),
    )(
        memory,
        features.T,
        dest.reshape(1, EVENTS),
        slot.reshape(1, EVENTS),
        neighbours.T,
        w_message,
        w_input,
        w_hidden,
        w_query,
        w_keyval,
        w_output,
    )


def solution(mesh):
    rows = P(("group", "dev"), None)
    placed = (rows, rows, rows, P(("group", "dev")), rows) + (P(),) * 6
    return jax.shard_map(
        body, mesh=mesh, in_specs=placed, out_specs=(rows, rows), check_vma=False
    )
```

time: 79.7 us -> 67.4 us (0.85)
  Pallas kernels: 75.3 us -> 62.7 us
    pallas_call x1, Pallas kernels: 75.3 us -> 62.7 us  [body(): pl.pallas_call(kernel, out_shape=(jax.ShapeDtypeStruct((CELLS, WIDTH), BF...]
where the time goes in v2:
time: 67.4 us; the launch traced here: 66.7 us
  Pallas kernels  62.7 us (93%)
  local copies, waits for them, and re-layouts  3.34 us (5%)
    pallas_call x1, Pallas kernels, body(): pl.pallas_call(kernel, out_shape=(jax.ShapeDtypeStruct((CELLS, WIDTH), BF...  62.7 us
    unnamed x2, local copies, waits for them, and re-layouts  3.34 us

profile of v2, /device:TPU:97, one launch (start us, length us, event | category | flops | bytes accessed | tf_op | source)
XLA Modules:
  0.0 66.7 jit_solution(2783681473243930266)
XLA Ops:
  0.6 62.7 %shard_map.122 = (bf16[256,512]{1,0:T(8,128)(2,1)}, bf16[256,512]{1,0:T(8,128)(2,1)}) custom-call(bf16[256,512]{1,0:T(8,128)(2,1)} %mem_ref.1, bf16[172,512]{1,0:T(8,128)(2,1)} %bitcast.4, s32[1,512]{1,0:T(1,128)} %bitcast.6, s32[1,512]{1,0:T(1,128)} %bitcast.7, s32[20,256]{1,0:T(8,128)} %bitcast.5, bf16[172,512]{1,0:T(8,128)(2,1)} %wmsg_ref.1, ...), custom_call_target="tpu_custom_call" | custom-call | flops 12000000000 | bytes 6000000 | tf_op jit(solution)/shard_map/pallas_call | solution.py:528
  63.4 1.7 %copy.15 = bf16[256,512]{1,0:T(8,128)(2,1)} copy(bf16[256,512]{1,0:T(8,128)(2,1)} %get-tuple-element.4) | data formatting | bytes 524288
  65.0 1.7 %copy.16 = bf16[256,512]{1,0:T(8,128)(2,1)} copy(bf16[256,512]{1,0:T(8,128)(2,1)} %get-tuple-element.5) | data formatting | bytes 524288

commit v3 on v2

--- a/solution.py
+++ b/solution.py
@@ -27,7 +27,10 @@
 RANGES = 16
 BUCKETS = OWNERS * ROLES
 TILE = 256
-LAG = 5
+LAG = 7
+EARLY = ((16, 0, 10),)
+LAST = (10, 16)
+LOWEST = -3.0e38
 BATCH = 4
 
 ORDER = (
@@ -135,13 +138,12 @@
 
 
 def kernel(
-    mem_ref, feat_ref, dest_ref, slot_ref, nbr_ref, wmsg_ref,
-    win_hbm, whid_hbm, wq_hbm, wkv_hbm, wout_hbm,
-    new_ref, emb_ref,
-    win, whid, wq, wkv, wout,
+    mem_hbm, feat_hbm, dest_hbm, slot_hbm, nbr_hbm, wmsg_hbm, win_hbm, whid_hbm, wq_hbm, wkv_hbm,
+    new_ref, att_ref,
+    mem_ref, feat_ref, dest_ref, slot_ref, nbr_ref, wmsg_ref, win, whid, wqkv, order,
     tail, wtail, ev_out, ev_in, gh, sums, cnt,
     mean_msg, w_both, row_hot, cell_hot, bkt, wanted, table, ind, tabs, reqs, celltab, cmat,
-    blocks, picks, to_left, to_right, q_ref, vals, scores, probs,
+    stats, blocks, picks, to_left, to_right, q_ref, vals, scores, probs, widen_all,
     w_sem, ev_send, ev_recv, rq_send, rq_recv, bl_send, bl_recv, pk_send, pk_recv,
 ):
     group, dev = lax.axis_index("group"), lax.axis_index("dev")
@@ -156,6 +158,9 @@
 
     barrier = pltpu.get_barrier_semaphore()
 
+    for side in (left, right):
+        pl.semaphore_signal(barrier, inc=1, device_id=(side, dev), device_id_type=MESH)
+
     def greet(k, _):
         pl.semaphore_signal(
             barrier, inc=1, device_id=(group, owner(k // SIDE, k % SIDE)), device_id_type=MESH
@@ -163,17 +168,29 @@
         return 0
 
     lax.fori_loop(1, OWNERS, greet, 0)
-    for side in (left, right):
-        pl.semaphore_signal(barrier, inc=1, device_id=(side, dev), device_id_type=MESH)
 
     loads = [
         pltpu.make_async_copy(src, dst, w_sem.at[i])
         for i, (src, dst) in enumerate(
-            ((whid_hbm, whid), (win_hbm, win), (wq_hbm, wq), (wkv_hbm, wkv), (wout_hbm, wout))
+            (
+                (whid_hbm, whid),
+                (win_hbm, win),
+                (wq_hbm, wqkv.at[0]),
+                (wkv_hbm.at[:, pl.ds(0, WIDTH)], wqkv.at[1]),
+                (wkv_hbm.at[:, pl.ds(WIDTH, WIDTH)], wqkv.at[2]),
+                (feat_hbm, feat_ref),
+                (dest_hbm, dest_ref),
+                (slot_hbm, slot_ref),
+                (nbr_hbm, nbr_ref),
+                (mem_hbm, mem_ref),
+                (wmsg_hbm, wmsg_ref),
+            )
         )
     ]
-    for load in loads:
+    for load in loads[5:] + loads[:5]:
         load.start()
+    for load in loads[5:8]:
+        load.wait()
 
     tail[...] = jnp.zeros_like(tail)
     tail[0:TAIL, :] = feat_ref[128:FEAT, :].astype(F32)
@@ -229,6 +246,7 @@
 
     lax.fori_loop(0, OWNERS - 1, send_events, 0)
 
+    loads[8].wait()
     ids = nbr_ref[...]
     role = ((ids >> 12) - group + 1 + RANGES) % RANGES
     named = (ids >> 8) & 15
@@ -283,23 +301,34 @@
     for ask in asks:
         ask.start()
 
-    def chosen(tab, column):
-        select = ones_where(iota((LANES, CELLS), 0) == column)
-        values = dot(tab[0:ROWS, :], select)
-        return ones_where(values == (iota((ROWS, CELLS), 1) + 1).astype(F32))
-
-    def cell_matrix(s, _):
-        for r in range(ROLES):
-            row = celltab[pl.ds(s * ROLES + r, 1), :]
-            hot = ones_where((iota((CELLS, LANES), 0) + 1).astype(F32) == row)
-            cmat[s, :, r * LANES : (r + 1) * LANES] = hot
-            cell_hot[s, r * ROWS : (r + 1) * ROWS, :] = chosen(tabs, BUCKETS + s * ROLES + r)
-            vals[s, r * LANES + ROWS : (r + 1) * LANES, :] = jnp.zeros((LANES - ROWS, WIDTH), BF16)
-        row_hot[s, 2 * ROWS : 3 * ROWS, :] = chosen(tabs, s * ROLES + 1)
-        return 0
-
-    lax.fori_loop(0, OWNERS, cell_matrix, 0)
-    scores[...] = jnp.zeros_like(scores)
+    every = jnp.ones((LANES, CELLS), BF16)
+
+    def chosen(*wanted):
+        lane = iota((ROWS, LANES), 1)
+        columns = [
+            jnp.where(lane == column, tab[0:ROWS, :].astype(F32), 0.0).astype(BF16)
+            for tab, column in wanted
+        ]
+        rows = ROWS * len(columns)
+        values = dot(jnp.concatenate(columns, axis=0), every)
+        return ones_where(values == (iota((rows, CELLS), 1) + 1).astype(F32))
+
+    def own_tables(i, _):
+        for s in (2 * i, 2 * i + 1):
+            first = s * ROLES
+            hot = chosen(
+                (tabs, BUCKETS + first),
+                (tabs, BUCKETS + first + 1),
+                (tabs, BUCKETS + first + 2),
+                (tabs, first + 1),
+            )
+            cell_hot[s] = hot[0 : ROLES * ROWS]
+            row_hot[s, 2 * ROWS : 3 * ROWS, :] = hot[ROLES * ROWS :]
+        return 0
+
+    lax.fori_loop(0, OWNERS // 2, own_tables, 0)
+    loads[9].wait()
+    loads[10].wait()
     loads[0].wait()
 
     def hidden(part, _):
@@ -308,6 +337,19 @@
         return 0
 
     lax.fori_loop(0, 3, hidden, 0)
+
+    column = iota((1, WIDTH), 1)
+    order[...] = ones_where(
+        iota((WIDTH, WIDTH), 0) == (column % HEADS) * HEAD + column // HEADS
+    )
+    for load in loads[2:5]:
+        load.wait()
+
+    def reorder(part, _):
+        wqkv[part] = dot(wqkv[part], order[...]).astype(BF16)
+        return 0
+
+    lax.fori_loop(0, 3, reorder, 0)
 
     wtail[...] = jnp.zeros_like(wtail)
     wtail[0:TAIL, :] = wmsg_ref[128:FEAT, :].astype(F32)
@@ -335,7 +377,8 @@
             main = ev_in[pl.ds(first, 8), part * HALF : (part + 1) * HALF, :]
             main = main.reshape(8 * HALF, 128)
             raw = dot(jnp.concatenate([main, tail_in], axis=1), w_both[part])
-            message = (raw * sigmoid(raw)).astype(BF16)
+            half = 0.5 * raw
+            message = (half + half * jnp.tanh(half)).astype(BF16)
             column = ones_where(iota((16, 128), 1) == 64 * part + TAIL)
             marks = dot_nt(column, tail_in)[0:1, :]
             here = (iota((CELLS, 8 * HALF), 0) + 1).astype(F32) == marks
@@ -381,7 +424,7 @@
             src_ref=source.at[s],
             dst_ref=picks.at[s, pl.ds(first, ROWS)],
             send_sem=pk_send.at[side],
-            recv_sem=pk_recv.at[s // 2],
+            recv_sem=pk_recv.at[(s + 1) // 2],
             device_id=(target, dev),
             device_id_type=MESH,
         )
@@ -396,21 +439,136 @@
 
     for number in START:
         bl_copy(number).start()
-    loads[2].wait()
-    q_ref[...] = (dot(blocks[0], wq[...]) * (HEAD**-0.5)).astype(BF16)
+    q_ref[...] = (dot(blocks[0], wqkv[0]) * (HEAD**-0.5)).astype(BF16)
 
     for ask in asks:
         ask.wait_recv()
 
-    def requested(s, _):
-        row_hot[s, 0:ROWS, :] = chosen(reqs.at[1], s * ROLES)
-        row_hot[s, ROWS : 2 * ROWS, :] = chosen(reqs.at[0], s * ROLES + 2)
-        return 0
-
-    lax.fori_loop(0, OWNERS, requested, 0)
-    loads[3].wait()
-
-    head_rows = ones_where(iota((16, WIDTH), 0) == iota((16, WIDTH), 1) // HEAD)
+    def requested(i, _):
+        for s in (2 * i, 2 * i + 1):
+            row_hot[s, 0 : 2 * ROWS, :] = chosen(
+                (reqs.at[1], s * ROLES), (reqs.at[0], s * ROLES + 2)
+            )
+            for r in range(ROLES):
+                row = celltab[pl.ds(s * ROLES + r, 1), :]
+                hot = ones_where((iota((CELLS, LANES), 0) + 1).astype(F32) == row)
+                cmat[s, :, r * LANES : (r + 1) * LANES] = hot
+                vals[s, r * LANES + ROWS : (r + 1) * LANES, :] = blank_rows
+        return 0
+
+    blank_rows = jnp.zeros((LANES - ROWS, WIDTH), BF16)
+    lax.fori_loop(0, OWNERS // 2, requested, 0)
+
+    head_rows = ones_where(iota((16, 2 * LANES), 1) % HEADS == iota((16, 2 * LANES), 0))
+
+    widen = ones_where(iota((HEADS, WIDTH), 0) == iota((HEADS, WIDTH), 1) % HEADS)
+    group_heads = 2 * ROLES * HEADS
+    lane = iota((group_heads, 2 * ROLES * LANES), 1)
+    head_of = lane // LANES * HEADS + lane % HEADS
+    widen_all[...] = ones_where(iota((group_heads, 2 * ROLES * LANES), 0) == head_of)
+
+    def entries(j):
+        return pl.ds(pl.multiple_of(j * CELLS, CELLS), CELLS)
+
+    def attend(begin, end):
+        low, high = begin * ROLES, end * ROLES
+        rows = slice(low * HEADS, high * HEADS)
+        part = scores[rows, :]
+        upper_part = part.astype(BF16)
+        lower_part = (part - upper_part.astype(F32)).astype(BF16)
+        parts = jnp.concatenate([upper_part, lower_part], axis=1)
+        numbers = lax.broadcasted_iota(I32, (high - low, HEADS, CELLS), 0) + low
+
+        def order_by_cell(i, top):
+            for j in range(BATCH):
+                j = i * BATCH + j
+                found = dot(parts, ind[:, entries(j)]).reshape(high - low, HEADS, CELLS)
+                bucket = bkt[pl.ds(j, 1), :]
+                inside = numbers == bucket.reshape(1, 1, CELLS)
+                mine = jnp.sum(jnp.where(inside, found, 0.0), axis=0)
+                mine = jnp.where(jnp.logical_and(bucket >= low, bucket < high), mine, LOWEST)
+                probs[j] = mine
+                top = jnp.maximum(top, mine)
+            return top
+
+        lowest = jnp.full((HEADS, CELLS), LOWEST, F32)
+        top = lax.fori_loop(0, NBR // BATCH, order_by_cell, lowest)
+        if begin > 0:
+            top = jnp.maximum(top, stats[0])
+        found = probs[...]
+        raised = jnp.where(found == LOWEST, 0.0, jnp.exp(found - top[None]))
+        total = jnp.sum(raised, axis=0)
+        if begin > 0:
+            scale = jnp.exp(stats[0] - top)
+            total = total + stats[1] * scale
+            if end == OWNERS:
+                inverse = 1.0 / total
+                raised = raised * inverse[None]
+                scale = scale * inverse
+            upper_part = scale.astype(BF16)
+            lower_part = (scale - upper_part.astype(F32)).astype(BF16)
+            sums[...] = sums[...] * (dot_tn(upper_part, widen) + dot_tn(lower_part, widen))
+        else:
+            sums[...] = jnp.zeros_like(sums)
+        stats[0] = top
+        stats[1] = total
+        probs[...] = raised
+        scores[rows, :] = jnp.zeros_like(part)
+
+        def order_by_bucket(i, _):
+            placed = []
+            for j in range(BATCH):
+                j = i * BATCH + j
+                inside = numbers == bkt[pl.ds(j, 1), :].reshape(1, 1, CELLS)
+                one = jnp.where(inside, probs[j][None], 0.0)
+                placed.append(one.reshape((high - low) * HEADS, CELLS).astype(BF16))
+            part = pl.ds(pl.multiple_of(i * BATCH * CELLS, BATCH * CELLS), BATCH * CELLS)
+            scores[rows, :] += dot_nt(jnp.concatenate(placed, axis=1), ind[0:LANES, part])
+            return 0
+
+        lax.fori_loop(0, NBR // BATCH, order_by_bucket, 0)
+
+        def weigh(i, _):
+            weighted = []
+            first = pl.multiple_of(i * group_heads, group_heads)
+            weights = scores[pl.ds(first, group_heads), :].T.astype(BF16)
+            wide = dot(weights, widen_all[...]).astype(BF16)
+            for r in range(2 * ROLES):
+                value = vals[2 * i + r // ROLES, (r % ROLES) * LANES : (r % ROLES + 1) * LANES, :]
+                weight = wide[:, r * LANES : (r + 1) * LANES]
+                weight = jnp.concatenate([weight] * (WIDTH // LANES), axis=1)
+                weighted.append(weight * value)
+            cells = jnp.concatenate([cmat[2 * i], cmat[2 * i + 1]], axis=1)
+            sums[...] += dot(cells, jnp.concatenate(weighted, axis=0))
+            return 0
+
+        lax.fori_loop(begin // 2, end // 2, weigh, 0)
+
+    def pick_rows(s):
+        got = dot(row_hot[s], blocks[s]).astype(BF16)
+        to_right[s] = got[0:ROWS]
+        pk_copy(0, s).start()
+        to_left[s] = got[ROWS : 2 * ROWS]
+        pk_copy(1, s).start()
+        picks[s, ROWS : 2 * ROWS, :] = got[2 * ROWS : 3 * ROWS]
+
+    def score_slots(t, number):
+        finish(to_left.at[pl.ds(0, 2 * number)], pk_recv.at[(t + 1) // 2])
+        picked = picks[pl.ds(t, number)].reshape(number * ROLES * ROWS, WIDTH)
+        owned = cell_hot[pl.ds(t, number)].reshape(number * ROLES * ROWS, CELLS)
+        keys = dot(picked, wqkv[1]).astype(BF16).astype(F32)
+        product = dot(owned, q_ref[...]) * keys
+        tiles = [product[:, i * LANES : (i + 1) * LANES] for i in range(WIDTH // LANES)]
+        product = (tiles[0] + tiles[1]) + (tiles[2] + tiles[3])
+        upper_part = product.astype(BF16)
+        lower_part = (product - upper_part.astype(F32)).astype(BF16)
+        split = jnp.concatenate([upper_part, lower_part], axis=1)
+        values = dot(picked, wqkv[2]).astype(BF16)
+        for r in range(number * ROLES):
+            rows = slice(r * ROWS, (r + 1) * ROWS)
+            first = pl.multiple_of((t * ROLES + r) * HEADS, HEADS)
+            scores[pl.ds(first, HEADS), 0:ROWS] = dot_nt(head_rows, split[rows])[0:HEADS]
+            vals[t + r // ROLES, (r % ROLES) * LANES : (r % ROLES) * LANES + ROWS, :] = values[rows]
 
     def step(s, _):
         @pl.when(s < OWNERS)
@@ -424,94 +582,28 @@
                         for number in sent:
                             bl_copy(number).start()
 
-            got = dot(row_hot[s], blocks[s]).astype(BF16)
-            to_right[s] = got[0:ROWS]
-            pk_copy(0, s).start()
-            to_left[s] = got[ROWS : 2 * ROWS]
-            pk_copy(1, s).start()
-            picks[s, ROWS : 2 * ROWS, :] = got[2 * ROWS : 3 * ROWS]
-
-        @pl.when(jnp.logical_and(s >= LAG, s % 2 == 1))
+            pick_rows(s)
+
+        for after, begin, end in EARLY:
+
+            @pl.when(s == after)
+            def _(begin=begin, end=end):
+                attend(begin, end)
+
+        @pl.when(jnp.logical_and(jnp.logical_and(s >= LAG, s < OWNERS + LAG - 2), s % 2 == 1))
         def _():
-            t = s - LAG
-            finish(to_left.at[pl.ds(0, 4)], pk_recv.at[t // 2])
-            picked = picks[pl.ds(t, 2)].reshape(2 * ROLES * ROWS, WIDTH)
-            keys = dot(picked, wkv[:, 0:WIDTH]).astype(BF16).astype(F32)
-            owned = cell_hot[pl.ds(t, 2)].reshape(2 * ROLES * ROWS, CELLS)
-            product = dot(owned, q_ref[...]) * keys
-            upper_part = product.astype(BF16)
-            lower_part = (product - upper_part.astype(F32)).astype(BF16)
-            for r in range(2 * ROLES):
-                rows = slice(r * ROWS, (r + 1) * ROWS)
-                score = dot_nt(head_rows, upper_part[rows]) + dot_nt(head_rows, lower_part[rows])
-                first = pl.multiple_of((t * ROLES + r) * HEADS, HEADS)
-                scores[pl.ds(first, HEADS), 0:ROWS] = score[0:HEADS]
-            values = dot(picked, wkv[:, WIDTH:]).astype(BF16)
-            for r in range(2 * ROLES):
-                vals[t + r // ROLES, (r % ROLES) * LANES : (r % ROLES) * LANES + ROWS, :] = values[
-                    r * ROWS : (r + 1) * ROWS
-                ]
+            score_slots(s - LAG + 1, 2)
+
+        @pl.when(jnp.logical_or(s == LAG - 1, s == OWNERS + LAG - 2))
+        def _():
+            score_slots((s // OWNERS) * (OWNERS - 1), 1)
 
         return 0
 
     lax.fori_loop(0, OWNERS + LAG - 1, step, 0)
 
-    all_scores = scores[...]
-    upper_part = all_scores.astype(BF16)
-    lower_part = (all_scores - upper_part.astype(F32)).astype(BF16)
-    parts = jnp.concatenate([upper_part, lower_part], axis=1)
-    numbers = lax.broadcasted_iota(I32, (BUCKETS, HEADS, CELLS), 0)
-
-    def entries(j):
-        return pl.ds(pl.multiple_of(j * CELLS, CELLS), CELLS)
-
-    def order_by_cell(i, top):
-        for j in range(BATCH):
-            j = i * BATCH + j
-            found = dot(parts, ind[:, entries(j)]).reshape(BUCKETS, HEADS, CELLS)
-            inside = numbers == bkt[pl.ds(j, 1), :].reshape(1, 1, CELLS)
-            mine = jnp.sum(jnp.where(inside, found, 0.0), axis=0)
-            probs[j] = mine
-            top = jnp.maximum(top, mine)
-        return top
-
-    lowest = jnp.full((HEADS, CELLS), -jnp.inf, F32)
-    top = lax.fori_loop(0, NBR // BATCH, order_by_cell, lowest)
-    raised = jnp.exp(probs[...] - top[None])
-    probs[...] = (raised * (1.0 / jnp.sum(raised, axis=0))[None]).astype(BF16).astype(F32)
-    scores[...] = jnp.zeros_like(scores)
-
-    def order_by_bucket(i, _):
-        placed = []
-        for j in range(BATCH):
-            j = i * BATCH + j
-            inside = numbers == bkt[pl.ds(j, 1), :].reshape(1, 1, CELLS)
-            one = jnp.where(inside, probs[j][None], 0.0).reshape(BUCKETS * HEADS, CELLS)
-            placed.append(one.astype(BF16))
-        part = pl.ds(pl.multiple_of(i * BATCH * CELLS, BATCH * CELLS), BATCH * CELLS)
-        scores[...] += dot_nt(jnp.concatenate(placed, axis=1), ind[0:LANES, part])
-        return 0
-
-    lax.fori_loop(0, NBR // BATCH, order_by_bucket, 0)
-
-    sums[...] = jnp.zeros_like(sums)
-    widen = ones_where(iota((HEADS, WIDTH), 0) == iota((HEADS, WIDTH), 1) // HEAD)
-
-    def weigh(i, _):
-        weighted = []
-        for r in range(2 * ROLES):
-            first = pl.multiple_of((2 * i * ROLES + r) * HEADS, HEADS)
-            wide = dot_tn(scores[pl.ds(first, HEADS), :].astype(BF16), widen)
-            value = vals[2 * i + r // ROLES, (r % ROLES) * LANES : (r % ROLES + 1) * LANES, :]
-            weighted.append((wide * value.astype(F32)).astype(BF16))
-        cells = jnp.concatenate([cmat[2 * i], cmat[2 * i + 1]], axis=1)
-        sums[...] += dot(cells, jnp.concatenate(weighted, axis=0))
-        return 0
-
-    lax.fori_loop(0, OWNERS // 2, weigh, 0)
-    attended = sums[...].astype(BF16)
-    loads[4].wait()
-    emb_ref[...] = (blocks[0].astype(F32) + dot(attended, wout[...])).astype(BF16)
+    attend(*LAST)
+    att_ref[...] = dot_nt(sums[...].astype(BF16), order[...]).astype(BF16)
 
     finish(ev_out.at[pl.ds(1, OWNERS - 1)], ev_send.at[0])
     for ask in asks:
@@ -521,23 +613,34 @@
     finish(to_left, pk_send.at[1])
 
 
+def embed(new_in, att_ref, wout_ref, new_ref, emb_ref):
+    new_memory = new_in[...]
+    new_ref[...] = new_memory
+    emb_ref[...] = (new_memory.astype(F32) + dot(att_ref[...], wout_ref[...])).astype(BF16)
+
+
 def body(memory, features, dest, slot, neighbours, w_message, w_input, w_hidden, w_query, w_keyval, w_output):
     inside = pl.BlockSpec(memory_space=pltpu.VMEM)
     outside = pl.BlockSpec(memory_space=pl.ANY)
     vmem, dma = pltpu.VMEM, pltpu.SemaphoreType.DMA
-    return pl.pallas_call(
+    new_memory, attended = pl.pallas_call(
         kernel,
         out_shape=(
             jax.ShapeDtypeStruct((CELLS, WIDTH), BF16),
             jax.ShapeDtypeStruct((CELLS, WIDTH), BF16),
         ),
-        in_specs=[inside] * 6 + [outside] * 5,
+        in_specs=[outside] * 10,
         out_specs=(inside, inside),
         scratch_shapes=[
+            vmem((CELLS, WIDTH), BF16),
+            vmem((FEAT, EVENTS), BF16),
+            vmem((1, EVENTS), I32),
+            vmem((1, EVENTS), I32),
+            vmem((NBR, CELLS), I32),
+            vmem((FEAT, WIDTH), BF16),
             vmem((WIDTH, 3 * WIDTH), BF16),
             vmem((WIDTH, 3 * WIDTH), BF16),
-            vmem((WIDTH, WIDTH), BF16),
-            vmem((WIDTH, 2 * WIDTH), BF16),
+            vmem((3, WIDTH, WIDTH), BF16),
             vmem((WIDTH, WIDTH), BF16),
             vmem((64, EVENTS), F32),
             vmem((64, WIDTH), F32),
@@ -558,6 +661,7 @@
             vmem((2, LANES, LANES), BF16),
             vmem((BUCKETS, LANES), F32),
             vmem((OWNERS, CELLS, ROLES * LANES), BF16),
+            vmem((2, HEADS, CELLS), F32),
             vmem((OWNERS, CELLS, WIDTH), BF16),
             vmem((OWNERS, ROLES * ROWS, WIDTH), BF16),
             vmem((OWNERS, ROWS, WIDTH), BF16),
@@ -566,7 +670,8 @@
             vmem((OWNERS, ROLES * LANES, WIDTH), BF16),
             vmem((BUCKETS * HEADS, LANES), F32),
             vmem((NBR, HEADS, CELLS), F32),
-            dma((5,)),
+            vmem((2 * ROLES * HEADS, 2 * ROLES * LANES), BF16),
+            dma((11,)),
             dma((1,)),
             dma((2,)),
             dma((2,)),
@@ -574,7 +679,7 @@
             dma((1,)),
             dma((len(GROUPS),)),
             dma((2,)),
-            dma((OWNERS // 2,)),
+            dma((OWNERS // 2 + 1,)),
         ],
         compiler_params=pltpu.CompilerParams(
             collective_id=0, has_side_effects=True, vmem_limit_bytes=58 * 1024 * 1024
@@ -593,8 +698,16 @@
         w_hidden,
         w_query,
         w_keyval,
-        w_output,
     )
+    return pl.pallas_call(
+        embed,
+        out_shape=(
+            jax.ShapeDtypeStruct((CELLS, WIDTH), BF16),
+            jax.ShapeDtypeStruct((CELLS, WIDTH), BF16),
+        ),
+        in_specs=[inside] * 3,
+        out_specs=(inside, inside),
+    )(new_memory, attended, w_output)
 
 
 def solution(mesh):

time: 67.4 us -> 62.7 us (0.930)
  local copies, waits for them, and re-layouts: 3.34 us -> 0 us
  Pallas kernels: 62.7 us -> 61.9 us
    unnamed x2 -> x0, local copies, waits for them, and re-layouts: 3.34 us -> none
    pallas_call x1, Pallas kernels: 62.7 us -> 59.7 us  [body(): pl.pallas_call(kernel, out_shape=(jax.ShapeDtypeStruct((CELLS, WIDTH), BF...]
    pallas_call x0 -> x1, Pallas kernels: none -> 2.21 us  [body(): pl.pallas_call(embed, out_shape=(jax.ShapeDtypeStruct((CELLS, WIDTH), BF1...]
where the time goes in v3:
time: 62.7 us; the launch traced here: 62.6 us
  Pallas kernels  61.9 us (99%)
  between operations  0.64 us (1%)
    pallas_call x1, Pallas kernels, body(): pl.pallas_call(kernel, out_shape=(jax.ShapeDtypeStruct((CELLS, WIDTH), BF...  59.7 us
    pallas_call x1, Pallas kernels, body(): pl.pallas_call(embed, out_shape=(jax.ShapeDtypeStruct((CELLS, WIDTH), BF1...  2.21 us

profile of v3, /device:TPU:97, one launch (start us, length us, event | category | flops | bytes accessed | tf_op | source)
XLA Modules:
  0.0 62.6 jit_solution(4472737660169751371)
XLA Ops:
  0.6 59.7 %shard_map.122 = (bf16[256,512]{1,0:T(8,128)(2,1)}, bf16[256,512]{1,0:T(8,128)(2,1)}) custom-call(bf16[256,512]{1,0:T(8,128)(2,1)} %mem_hbm.1, bf16[172,512]{1,0:T(8,128)(2,1)} %bitcast.4, s32[1,512]{1,0:T(1,128)} %bitcast.6, s32[1,512]{1,0:T(1,128)} %bitcast.7, s32[20,256]{1,0:T(8,128)} %bitcast.5, bf16[172,512]{1,0:T(8,128)(2,1)} %wmsg_hbm.1, ...), custom_call_target="tpu_custom_call" | custom-call | flops 12000000000 | bytes 6000000 | tf_op jit(solution)/shard_map/pallas_call | solution.py:626
  60.4 2.2 %shard_map.123 = (bf16[256,512]{1,0:T(8,128)(2,1)}, bf16[256,512]{1,0:T(8,128)(2,1)}) custom-call(bf16[256,512]{1,0:T(8,128)(2,1)} %get-tuple-element.4.new_in, bf16[256,512]{1,0:T(8,128)(2,1)} %get-tuple-element.5.att_ref, bf16[512,512]{1,0:T(8,128)(2,1)} %wout_ref.1), custom_call_target="tpu_custom_call" | custom-call | tf_op jit(solution)/shard_map/pallas_call | solution.py:702

commit v4 on v3

--- a/solution.py
+++ b/solution.py
@@ -138,9 +138,9 @@
 
 
 def kernel(
-    mem_hbm, feat_hbm, dest_hbm, slot_hbm, nbr_hbm, wmsg_hbm, win_hbm, whid_hbm, wq_hbm, wkv_hbm,
-    new_ref, att_ref,
-    mem_ref, feat_ref, dest_ref, slot_ref, nbr_ref, wmsg_ref, win, whid, wqkv, order,
+    mem_hbm, feat_hbm, dest_hbm, slot_hbm, nbr_hbm, wmsg_hbm, win_hbm, whid_hbm, wq_hbm, wkv_hbm, wout_hbm,
+    new_ref, emb_ref,
+    mem_ref, feat_ref, dest_ref, slot_ref, nbr_ref, wmsg_ref, win, whid, wqkv, order, wout,
     tail, wtail, ev_out, ev_in, gh, sums, cnt,
     mean_msg, w_both, row_hot, cell_hot, bkt, wanted, table, ind, tabs, reqs, celltab, cmat,
     stats, blocks, picks, to_left, to_right, q_ref, vals, scores, probs, widen_all,
@@ -153,6 +153,10 @@
     def owner(dy, dx):
         return ((y + dy) % SIDE) * SIDE + (x + dx) % SIDE
 
+    def event_owner(k):
+        dy = k % 8 // 2
+        return owner(dy, k % 2 * 2 + (dy + k // 8) % 2)
+
     def finish(part, sem):
         pltpu.make_async_copy(part, part, sem).wait()
 
@@ -163,7 +167,7 @@
 
     def greet(k, _):
         pl.semaphore_signal(
-            barrier, inc=1, device_id=(group, owner(k // SIDE, k % SIDE)), device_id_type=MESH
+            barrier, inc=1, device_id=(group, event_owner(k)), device_id_type=MESH
         )
         return 0
 
@@ -184,6 +188,7 @@
                 (nbr_hbm, nbr_ref),
                 (mem_hbm, mem_ref),
                 (wmsg_hbm, wmsg_ref),
+                (wout_hbm, wout.at[0]),
             )
         )
     ]
@@ -214,7 +219,7 @@
             dst_ref=ev_in.at[k],
             send_sem=ev_send.at[0],
             recv_sem=ev_recv.at[k // 8],
-            device_id=(group, owner(k // SIDE, k % SIDE)),
+            device_id=(group, event_owner(k)),
             device_id_type=MESH,
         )
 
@@ -223,7 +228,7 @@
         packed = []
         for part in range(2):
             pick = [
-                iota((HALF, EVENTS), 0) == place - (owner(rows, column) * CAP + part * HALF)
+                iota((HALF, EVENTS), 0) == place - (event_owner(rows * SIDE + column) * CAP + part * HALF)
                 for column in range(SIDE)
             ]
             pick = jnp.concatenate([ones_where(one) for one in pick], axis=0)
@@ -244,7 +249,7 @@
         ev_copy(OWNERS - 1 - i).start()
         return 0
 
-    lax.fori_loop(0, OWNERS - 1, send_events, 0)
+    lax.fori_loop(0, 8, send_events, 0)
 
     loads[8].wait()
     ids = nbr_ref[...]
@@ -284,6 +289,7 @@
         return offset
 
     lax.fori_loop(0, NBR // BATCH, tabulate, jnp.zeros((BUCKETS, 1), F32))
+    lax.fori_loop(8, OWNERS - 1, send_events, 0)
     tabs[...] = table[...].astype(BF16)
     celltab[...] = table[...].T[BUCKETS : 2 * BUCKETS, :]
 
@@ -441,6 +447,8 @@
         bl_copy(number).start()
     q_ref[...] = (dot(blocks[0], wqkv[0]) * (HEAD**-0.5)).astype(BF16)
 
+    loads[11].wait()
+    wout[1] = dot_tn(order[...], wout[0]).astype(BF16)
     for ask in asks:
         ask.wait_recv()
 
@@ -603,7 +611,8 @@
     lax.fori_loop(0, OWNERS + LAG - 1, step, 0)
 
     attend(*LAST)
-    att_ref[...] = dot_nt(sums[...].astype(BF16), order[...]).astype(BF16)
+    attended = sums[...].astype(BF16)
+    emb_ref[...] = (blocks[0].astype(F32) + dot(attended, wout[1])).astype(BF16)
 
     finish(ev_out.at[pl.ds(1, OWNERS - 1)], ev_send.at[0])
     for ask in asks:
@@ -613,23 +622,22 @@
     finish(to_left, pk_send.at[1])
 
 
-def embed(new_in, att_ref, wout_ref, new_ref, emb_ref):
-    new_memory = new_in[...]
-    new_ref[...] = new_memory
-    emb_ref[...] = (new_memory.astype(F32) + dot(att_ref[...], wout_ref[...])).astype(BF16)
+def hand_over(new_in, emb_in, new_ref, emb_ref):
+    new_ref[...] = new_in[...]
+    emb_ref[...] = emb_in[...]
 
 
 def body(memory, features, dest, slot, neighbours, w_message, w_input, w_hidden, w_query, w_keyval, w_output):
     inside = pl.BlockSpec(memory_space=pltpu.VMEM)
     outside = pl.BlockSpec(memory_space=pl.ANY)
     vmem, dma = pltpu.VMEM, pltpu.SemaphoreType.DMA
-    new_memory, attended = pl.pallas_call(
+    results = pl.pallas_call(
         kernel,
         out_shape=(
             jax.ShapeDtypeStruct((CELLS, WIDTH), BF16),
             jax.ShapeDtypeStruct((CELLS, WIDTH), BF16),
         ),
-        in_specs=[outside] * 10,
+        in_specs=[outside] * 11,
         out_specs=(inside, inside),
         scratch_shapes=[
             vmem((CELLS, WIDTH), BF16),
@@ -642,6 +650,7 @@
             vmem((WIDTH, 3 * WIDTH), BF16),
             vmem((3, WIDTH, WIDTH), BF16),
             vmem((WIDTH, WIDTH), BF16),
+            vmem((2, WIDTH, WIDTH), BF16),
             vmem((64, EVENTS), F32),
             vmem((64, WIDTH), F32),
             vmem((OWNERS, PACK, 128), BF16),
@@ -671,7 +680,7 @@
             vmem((BUCKETS * HEADS, LANES), F32),
             vmem((NBR, HEADS, CELLS), F32),
             vmem((2 * ROLES * HEADS, 2 * ROLES * LANES), BF16),
-            dma((11,)),
+            dma((12,)),
             dma((1,)),
             dma((2,)),
             dma((2,)),
@@ -698,16 +707,17 @@
         w_hidden,
         w_query,
         w_keyval,
+        w_output,
     )
     return pl.pallas_call(
-        embed,
+        hand_over,
         out_shape=(
             jax.ShapeDtypeStruct((CELLS, WIDTH), BF16),
             jax.ShapeDtypeStruct((CELLS, WIDTH), BF16),
         ),
-        in_specs=[inside] * 3,
+        in_specs=[inside] * 2,
         out_specs=(inside, inside),
-    )(new_memory, attended, w_output)
+    )(*results)
 
 
 def solution(mesh):

time: 62.7 us -> 61.9 us (0.987)
  Pallas kernels: 61.9 us -> 60.8 us
    pallas_call x1, Pallas kernels: 59.7 us -> 59 us  [body(): pl.pallas_call(kernel, out_shape=(jax.ShapeDtypeStruct((CELLS, WIDTH), BF...]
where the time goes in v4:
time: 61.9 us; the launch traced here: 61.5 us
  Pallas kernels  60.8 us (98%)
  between operations  0.64 us (1%)
    pallas_call x1, Pallas kernels, body(): pl.pallas_call(kernel, out_shape=(jax.ShapeDtypeStruct((CELLS, WIDTH), BF...  59 us
    pallas_call x1, Pallas kernels, body(): pl.pallas_call(hand_over, out_shape=(jax.ShapeDtypeStruct((CELLS, WIDTH),...  1.84 us

profile of v4, /device:TPU:97, one launch (start us, length us, event | category | flops | bytes accessed | tf_op | source)
XLA Modules:
  0.0 61.5 jit_solution(487603202499154067)
XLA Ops:
  0.6 59.0 %shard_map.122 = (bf16[256,512]{1,0:T(8,128)(2,1)}, bf16[256,512]{1,0:T(8,128)(2,1)}) custom-call(bf16[256,512]{1,0:T(8,128)(2,1)} %mem_hbm.1, bf16[172,512]{1,0:T(8,128)(2,1)} %bitcast.4, s32[1,512]{1,0:T(1,128)} %bitcast.6, s32[1,512]{1,0:T(1,128)} %bitcast.7, s32[20,256]{1,0:T(8,128)} %bitcast.5, bf16[172,512]{1,0:T(8,128)(2,1)} %wmsg_hbm.1, ...), custom_call_target="tpu_custom_call" | custom-call | flops 12000000000 | bytes 6000000 | tf_op jit(solution)/shard_map/pallas_call | solution.py:634
  59.6 1.8 %shard_map.123 = (bf16[256,512]{1,0:T(8,128)(2,1)}, bf16[256,512]{1,0:T(8,128)(2,1)}) custom-call(bf16[256,512]{1,0:T(8,128)(2,1)} %get-tuple-element.4.new_in, bf16[256,512]{1,0:T(8,128)(2,1)} %get-tuple-element.5.emb_in), custom_call_target="tpu_custom_call" | custom-call | tf_op jit(solution)/shard_map/pallas_call | solution.py:712

commit v5 on v4

--- a/solution.py
+++ b/solution.py
@@ -138,9 +138,9 @@
 
 
 def kernel(
-    mem_hbm, feat_hbm, dest_hbm, slot_hbm, nbr_hbm, wmsg_hbm, win_hbm, whid_hbm, wq_hbm, wkv_hbm, wout_hbm,
+    mem_hbm, feat_ref, dest_hbm, slot_hbm, nbr_hbm, wmsg_ref, win_hbm, whid_hbm, wq_hbm, wkv_hbm, wout_hbm,
     new_ref, emb_ref,
-    mem_ref, feat_ref, dest_ref, slot_ref, nbr_ref, wmsg_ref, win, whid, wqkv, order, wout,
+    mem_ref, dest_ref, slot_ref, nbr_ref, win, whid, wqkv, order, wout,
     tail, wtail, ev_out, ev_in, gh, sums, cnt,
     mean_msg, w_both, row_hot, cell_hot, bkt, wanted, table, ind, tabs, reqs, celltab, cmat,
     stats, blocks, picks, to_left, to_right, q_ref, vals, scores, probs, widen_all,
@@ -182,19 +182,17 @@
                 (wq_hbm, wqkv.at[0]),
                 (wkv_hbm.at[:, pl.ds(0, WIDTH)], wqkv.at[1]),
                 (wkv_hbm.at[:, pl.ds(WIDTH, WIDTH)], wqkv.at[2]),
-                (feat_hbm, feat_ref),
                 (dest_hbm, dest_ref),
                 (slot_hbm, slot_ref),
                 (nbr_hbm, nbr_ref),
                 (mem_hbm, mem_ref),
-                (wmsg_hbm, wmsg_ref),
                 (wout_hbm, wout.at[0]),
             )
         )
     ]
     for load in loads[5:] + loads[:5]:
         load.start()
-    for load in loads[5:8]:
+    for load in loads[5:7]:
         load.wait()
 
     tail[...] = jnp.zeros_like(tail)
@@ -251,7 +249,7 @@
 
     lax.fori_loop(0, 8, send_events, 0)
 
-    loads[8].wait()
+    loads[7].wait()
     ids = nbr_ref[...]
     role = ((ids >> 12) - group + 1 + RANGES) % RANGES
     named = (ids >> 8) & 15
@@ -333,8 +331,7 @@
         return 0
 
     lax.fori_loop(0, OWNERS // 2, own_tables, 0)
-    loads[9].wait()
-    loads[10].wait()
+    loads[8].wait()
     loads[0].wait()
 
     def hidden(part, _):
@@ -447,7 +444,7 @@
         bl_copy(number).start()
     q_ref[...] = (dot(blocks[0], wqkv[0]) * (HEAD**-0.5)).astype(BF16)
 
-    loads[11].wait()
+    loads[9].wait()
     wout[1] = dot_tn(order[...], wout[0]).astype(BF16)
     for ask in asks:
         ask.wait_recv()
@@ -637,15 +634,13 @@
             jax.ShapeDtypeStruct((CELLS, WIDTH), BF16),
             jax.ShapeDtypeStruct((CELLS, WIDTH), BF16),
         ),
-        in_specs=[outside] * 11,
+        in_specs=[outside, inside, outside, outside, outside, inside] + [outside] * 5,
         out_specs=(inside, inside),
         scratch_shapes=[
             vmem((CELLS, WIDTH), BF16),
-            vmem((FEAT, EVENTS), BF16),
             vmem((1, EVENTS), I32),
             vmem((1, EVENTS), I32),
             vmem((NBR, CELLS), I32),
-            vmem((FEAT, WIDTH), BF16),
             vmem((WIDTH, 3 * WIDTH), BF16),
             vmem((WIDTH, 3 * WIDTH), BF16),
             vmem((3, WIDTH, WIDTH), BF16),
@@ -680,7 +675,7 @@
             vmem((BUCKETS * HEADS, LANES), F32),
             vmem((NBR, HEADS, CELLS), F32),
             vmem((2 * ROLES * HEADS, 2 * ROLES * LANES), BF16),
-            dma((12,)),
+            dma((10,)),
             dma((1,)),
             dma((2,)),
             dma((2,)),

time: 61.9 us -> 62.3 us (level)
  no operation moved by 1% of the time
where the time goes in v5:
time: 62.3 us; the launch traced here: 62.1 us
  Pallas kernels  61.4 us (99%)
  between operations  0.64 us (1%)
    pallas_call x1, Pallas kernels, body(): pl.pallas_call(kernel, out_shape=(jax.ShapeDtypeStruct((CELLS, WIDTH), BF...  59.6 us
    pallas_call x1, Pallas kernels, body(): pl.pallas_call(hand_over, out_shape=(jax.ShapeDtypeStruct((CELLS, WIDTH),...  1.84 us

profile of v5, /device:TPU:97, one launch (start us, length us, event | category | flops | bytes accessed | tf_op | source)
XLA Modules:
  0.0 62.1 jit_solution(11934703659854133824)
XLA Ops:
  0.6 59.6 %shard_map.122 = (bf16[256,512]{1,0:T(8,128)(2,1)}, bf16[256,512]{1,0:T(8,128)(2,1)}) custom-call(bf16[256,512]{1,0:T(8,128)(2,1)} %mem_hbm.1, bf16[172,512]{1,0:T(8,128)(2,1)} %bitcast.4, s32[1,512]{1,0:T(1,128)} %bitcast.6, s32[1,512]{1,0:T(1,128)} %bitcast.7, s32[20,256]{1,0:T(8,128)} %bitcast.5, bf16[172,512]{1,0:T(8,128)(2,1)} %wmsg_ref.1, ...), custom_call_target="tpu_custom_call" | custom-call | flops 12000000000 | bytes 6000000 | tf_op jit(solution)/shard_map/pallas_call | solution.py:631
  60.2 1.8 %shard_map.123 = (bf16[256,512]{1,0:T(8,128)(2,1)}, bf16[256,512]{1,0:T(8,128)(2,1)}) custom-call(bf16[256,512]{1,0:T(8,128)(2,1)} %get-tuple-element.4.new_in, bf16[256,512]{1,0:T(8,128)(2,1)} %get-tuple-element.5.emb_in), custom_call_target="tpu_custom_call" | custom-call | tf_op jit(solution)/shard_map/pallas_call | solution.py:707
